TPU v7x, 32 devices: a whole 2x2x4 slice. The times are simulated.
32 devices in a mesh: dp: 8 (over z, x), tensor: 4 (over y, core).
Axes of the slice: x: 2, y: 2, z: 4, core: 2. Of those that a mesh axis runs over, the one named last changes fastest.
Arguments:
- tokens: bfloat16 [10976, 1280], P(('dp', 'tensor')), may hold values from -6 to 6
- grad_out: bfloat16 [10976, 1280], P(('dp', 'tensor')), may hold values from -6 to 6
- adapter_index: int32 [2], replicated, may hold values from 0 to 7
- norm1_gain: bfloat16 [1280], replicated, may hold values from 0.099609375 to 1.8984375
- norm1_shift: bfloat16 [1280], replicated, may hold values from -2.5 to 2.5
- qkv_weight: bfloat16 [1280, 3, 1280], P(None, None, 'tensor'), may hold values from -0.15625 to 0.15625
- qkv_bias: bfloat16 [3, 1280], P(None, 'tensor'), may hold values from -2.5 to 2.5
- rel_pos_h: bfloat16 [27, 80], replicated, may hold values from -1.25 to 1.25
- rel_pos_w: bfloat16 [27, 80], replicated, may hold values from -1.25 to 1.25
- proj_weight: bfloat16 [1280, 1280], P('tensor'), may hold values from -0.625 to 0.625
- proj_bias: bfloat16 [1280], replicated, may hold values from -2.5 to 2.5
- norm2_gain: bfloat16 [1280], replicated, may hold values from 0.099609375 to 1.8984375
- norm2_shift: bfloat16 [1280], replicated, may hold values from -2.5 to 2.5
- lin1_weight: bfloat16 [1280, 5120], P(None, 'tensor'), may hold values from -0.15625 to 0.15625
- lin1_bias: bfloat16 [5120], P('tensor'), may hold values from -2.5 to 2.5
- lin2_weight: bfloat16 [5120, 1280], P('tensor'), may hold values from -0.078125 to 0.078125
- lin2_bias: bfloat16 [1280], replicated, may hold values from -2.5 to 2.5
- qkv_down: bfloat16 [8, 1280, 16], replicated, may hold values from -0.15625 to 0.15625
- qkv_up: bfloat16 [8, 16, 3, 1280], P(None, None, None, 'tensor'), may hold values from -1.5 to 1.5
- proj_down: bfloat16 [8, 1280, 16], P(None, 'tensor'), may hold values from -0.625 to 0.625
- proj_up: bfloat16 [8, 16, 1280], replicated, may hold values from -1.5 to 1.5
- lin1_down: bfloat16 [8, 1280, 16], replicated, may hold values from -0.15625 to 0.15625
- lin1_up: bfloat16 [8, 16, 5120], P(None, None, 'tensor'), may hold values from -1.5 to 1.5
- lin2_down: bfloat16 [8, 5120, 16], P(None, 'tensor'), may hold values from -0.078125 to 0.078125
- lin2_up: bfloat16 [8, 16, 1280], replicated, may hold values from -1.5 to 1.5
Outputs:
- output: bfloat16 [10976, 1280], P(('dp', 'tensor'))
- grad_tokens: bfloat16 [10976, 1280], P(('dp', 'tensor'))
- grad_qkv_down: float32 [8, 1280, 16], replicated
- grad_qkv_up: float32 [8, 16, 3, 1280], P(None, None, None, 'tensor')
- grad_proj_down: float32 [8, 1280, 16], P(None, 'tensor')
- grad_proj_up: float32 [8, 16, 1280], replicated
- grad_lin1_down: float32 [8, 1280, 16], replicated
- grad_lin1_up: float32 [8, 16, 5120], P(None, None, 'tensor')
- grad_lin2_down: float32 [8, 5120, 16], P(None, 'tensor')
- grad_lin2_up: float32 [8, 16, 1280], replicated
Inputs may be any that keep to these rules, and one draw needn't show every extreme that they name: `adapter_index`: one adapter for each image.
All inputs are finite; a program needn't handle non-finite values.
Results may differ from a plain program's by a relative error of at most 0.019.
Values may be sent and summed in bfloat16 or wider, within the bound.
A program may use at most 256 MiB of HBM per device.

v0:
```python
import jax
import jax.numpy as jnp
from jax import lax
from jax.sharding import PartitionSpec as P

HEAD_DIM = 80
WIN = 14
SIDE = 64
RANK = 16
ADAPTERS = 8
WIN_DEV = 7
GROUP = 4
GRID = 5


HIGH = lax.Precision.HIGHEST
ADAPT = 0.5
EPS = 1e-06


def fast_dot(first_op, second_op):
    return jnp.dot(first_op, second_op, preferred_element_type=jnp.float32)


def trans_dot(first_op, second_op):
    return lax.dot_general(
        first_op, second_op, (((1,), (1,)), ((), ())), preferred_element_type=jnp.float32
    )


def exact_dot(first_op, second_op):
    return jnp.dot(first_op, second_op.astype(jnp.float32), precision=HIGH)


def cross_dot(first_op, second_op):
    return lax.dot_general(
        first_op.astype(jnp.float32),
        second_op.astype(jnp.float32),
        (((0,), (0,)), ((), ())),
        precision=HIGH,
    )


def window_mask(first_slot, count_all):
    position = jnp.arange(count_all, dtype=jnp.int32)
    slot_index = first_slot + position // (WIN * WIN)
    within = position % (WIN * WIN)
    image_row = slot_index // GRID * WIN + within // WIN
    image_col = slot_index % GRID * WIN + within % WIN
    inside = (slot_index < GRID * GRID) & (image_row < SIDE) & (image_col < SIDE)
    return jnp.where(inside, 1.0, 0.0).astype(jnp.float32)[:, None]


def offset_table(position_table):
    offsets = (jnp.arange(WIN)[:, None] - jnp.arange(WIN)[None, :] + WIN - 1).reshape(-1)
    one_hot = (offsets[:, None] == jnp.arange(2 * WIN - 1)[None, :]).astype(jnp.float32)
    return exact_dot(one_hot, position_table).reshape(WIN, WIN, -1).astype(jnp.bfloat16)


def norm_parts(values):
    row_mean = jnp.mean(values, axis=-1, keepdims=True)
    centered = values - row_mean
    inv_std = lax.rsqrt(jnp.mean(centered * centered, axis=-1, keepdims=True) + EPS)
    return (centered * inv_std, inv_std)


def norm_back(grad_in, normalized, inv_std, norm_gain):
    scaled = grad_in * norm_gain
    return inv_std * (
        scaled
        - jnp.mean(scaled, axis=-1, keepdims=True)
        - normalized * jnp.mean(scaled * normalized, axis=-1, keepdims=True)
    )


def window_scores(queries, key_win, table_h, table_w):
    win_count, head_count = (queries.shape[0], queries.shape[1])
    tokens_win = WIN * WIN
    base_scores = jnp.einsum(
        "nhqc,nhkc->nhqk",
        queries.reshape(win_count, head_count, tokens_win, -1),
        key_win.reshape(win_count, head_count, tokens_win, -1),
        preferred_element_type=jnp.float32,
    ) * HEAD_DIM ** (-0.5)
    rel_rows = jnp.einsum("nhabc,akc->nhabk", queries, table_h, preferred_element_type=jnp.float32)
    rel_cols = jnp.einsum("nhabc,bkc->nhabk", queries, table_w, preferred_element_type=jnp.float32)
    scores = (
        base_scores.reshape(win_count, head_count, WIN, WIN, WIN, WIN)
        + rel_rows[:, :, :, :, :, None]
        + rel_cols[:, :, :, :, None, :]
    )
    return scores.reshape(win_count, head_count, tokens_win, tokens_win)


def attention_back(queries, key_win, value_win, log_total, grad_att, table_h, table_w):
    win_count, head_count = (queries.shape[0], queries.shape[1])
    tokens_win = WIN * WIN
    probs = jnp.exp(window_scores(queries, key_win, table_h, table_w) - log_total)
    grad_rows = grad_att.reshape(win_count, head_count, tokens_win, -1)
    dprob = jnp.einsum(
        "nhqc,nhkc->nhqk",
        grad_rows,
        value_win.reshape(win_count, head_count, tokens_win, -1),
        preferred_element_type=jnp.float32,
    )
    dvalues = jnp.einsum(
        "nhqk,nhqc->nhkc", probs.astype(jnp.bfloat16), grad_rows, preferred_element_type=jnp.float32
    )
    inner_sum = jnp.sum(probs * dprob, axis=-1, keepdims=True)
    dscore = (probs * (dprob - inner_sum)).astype(jnp.bfloat16)
    dqueries = jnp.einsum(
        "nhqk,nhkc->nhqc",
        dscore,
        key_win.reshape(win_count, head_count, tokens_win, -1),
        preferred_element_type=jnp.float32,
    ) * HEAD_DIM ** (-0.5)
    dkeys = jnp.einsum(
        "nhqk,nhqc->nhkc",
        dscore,
        queries.reshape(win_count, head_count, tokens_win, -1),
        preferred_element_type=jnp.float32,
    ) * HEAD_DIM ** (-0.5)
    dscore_six = dscore.astype(jnp.float32).reshape(win_count, head_count, WIN, WIN, WIN, WIN)
    from_rows = jnp.einsum(
        "nhabk,akc->nhabc", jnp.sum(dscore_six, axis=5), table_h.astype(jnp.float32), precision=HIGH
    )
    from_cols = jnp.einsum(
        "nhabk,bkc->nhabc", jnp.sum(dscore_six, axis=4), table_w.astype(jnp.float32), precision=HIGH
    )
    dqueries = dqueries.reshape(queries.shape) + from_rows + from_cols
    return (
        dqueries.astype(jnp.bfloat16),
        dkeys.reshape(queries.shape).astype(jnp.bfloat16),
        dvalues.reshape(queries.shape).astype(jnp.bfloat16),
    )


def on_device(
    tokens,
    grad_out,
    adapter_index,
    norm1_gain,
    norm1_shift,
    qkv_weight,
    qkv_bias,
    rel_pos_h,
    rel_pos_w,
    proj_weight,
    proj_bias,
    norm2_gain,
    norm2_shift,
    lin1_weight,
    lin1_bias,
    lin2_weight,
    lin2_bias,
    qkv_down,
    qkv_up,
    proj_down,
    proj_up,
    lin1_down,
    lin1_up,
    lin2_down,
    lin2_up,
):
    tensor_size = lax.axis_size("tensor")
    row_count = tokens.shape[0]
    full_rows = row_count * tensor_size
    dp_place = lax.axis_index("dp")
    tensor_place = lax.axis_index("tensor")
    valid_full = window_mask(dp_place % GROUP * WIN_DEV, full_rows)
    valid_local = lax.dynamic_slice_in_dim(valid_full, tensor_place * row_count, row_count, 0)
    image_place = dp_place // GROUP
    pick = jnp.sum(jnp.where(jnp.arange(adapter_index.shape[0]) == image_place, adapter_index, 0))
    slot_hot = jnp.where(jnp.arange(ADAPTERS) == pick, 1.0, 0.0).astype(jnp.float32)

    def select(table_all):
        return lax.dynamic_index_in_dim(table_all, pick, 0, keepdims=False)

    def into_slot(term):
        return slot_hot.reshape((-1,) + (1,) * term.ndim) * term[None]

    head_local = qkv_weight.shape[2] // HEAD_DIM
    width_local = qkv_weight.shape[2]

    def to_windows(values):
        return values.reshape(-1, WIN, WIN, head_local, HEAD_DIM).transpose(0, 3, 1, 2, 4)

    def from_windows(values):
        return values.transpose(0, 2, 3, 1, 4).reshape(full_rows, -1)

    gain_one = norm1_gain.astype(jnp.float32)
    gain_two = norm2_gain.astype(jnp.float32)
    table_h = offset_table(rel_pos_h)
    table_w = offset_table(rel_pos_w)
    a_qkv = select(qkv_down)
    b_qkv = select(qkv_up).reshape(RANK, -1)
    a_proj = select(proj_down)
    b_proj = select(proj_up)
    a_lin1 = select(lin1_down)
    b_lin2 = select(lin2_up)
    qkv_flat = qkv_weight.reshape(qkv_weight.shape[0], -1)
    x_local = tokens.astype(jnp.float32)
    normal_one, inv_one = norm_parts(x_local)
    xn1_local = (valid_local * (normal_one * gain_one + norm1_shift.astype(jnp.float32))).astype(
        jnp.bfloat16
    )
    xn1 = lax.all_gather(xn1_local, "tensor", axis=0, tiled=True)
    down_q = fast_dot(xn1, a_qkv)
    qkv = (
        fast_dot(xn1, qkv_flat)
        + qkv_bias.astype(jnp.float32).reshape(-1)
        + ADAPT * exact_dot(down_q, b_qkv)
    )
    qkv = qkv.astype(jnp.bfloat16).reshape(full_rows, 3, width_local)
    queries = to_windows(qkv[:, 0])
    key_win = to_windows(qkv[:, 1])
    value_win = to_windows(qkv[:, 2])
    win_count = queries.shape[0]
    tokens_win = WIN * WIN
    scores = window_scores(queries, key_win, table_h, table_w)
    row_max = jnp.max(scores, axis=-1, keepdims=True)
    exponent = jnp.exp(scores - row_max)
    row_total = jnp.sum(exponent, axis=-1, keepdims=True)
    log_total = row_max + jnp.log(row_total)
    probs = exponent / row_total
    attended = jnp.einsum(
        "nhqk,nhkc->nhqc",
        probs.astype(jnp.bfloat16),
        value_win.reshape(win_count, head_local, tokens_win, -1),
        preferred_element_type=jnp.float32,
    )
    att = from_windows(attended.reshape(queries.shape)).astype(jnp.bfloat16)
    down_p = fast_dot(att, a_proj)
    down_part = down_p
    branch_a = lax.psum_scatter(
        (fast_dot(att, proj_weight) + ADAPT * exact_dot(down_part, b_proj)).astype(jnp.bfloat16),
        "tensor",
        scatter_dimension=0,
        tiled=True,
    ).astype(jnp.float32)
    middle = x_local + valid_local * (branch_a + proj_bias.astype(jnp.float32))
    normal_two, inv_two = norm_parts(middle)
    xn2_local = (normal_two * gain_two + norm2_shift.astype(jnp.float32)).astype(jnp.bfloat16)
    xn2 = lax.all_gather(xn2_local, "tensor", axis=0, tiled=True)
    w_lin1, c_lin1, b_lin1, a_lin2, w_lin2 = (
        lin1_weight,
        lin1_bias,
        select(lin1_up),
        select(lin2_down),
        lin2_weight,
    )
    down_1 = fast_dot(xn2, a_lin1)
    hidden_pre = (
        fast_dot(xn2, w_lin1) + c_lin1.astype(jnp.float32) + ADAPT * exact_dot(down_1, b_lin1)
    )
    gelu_value, gelu_grad = jax.vjp(
        lambda values: jax.nn.gelu(values, approximate=False), hidden_pre
    )
    hidden_act = gelu_value.astype(jnp.bfloat16)
    down_2 = fast_dot(hidden_act, a_lin2)
    down_part = down_2
    branch_m = lax.psum_scatter(
        (fast_dot(hidden_act, w_lin2) + ADAPT * exact_dot(down_part, b_lin2)).astype(jnp.bfloat16),
        "tensor",
        scatter_dimension=0,
        tiled=True,
    ).astype(jnp.float32)
    output = (middle + valid_local * (branch_m + lin2_bias.astype(jnp.float32))).astype(
        jnp.bfloat16
    )
    dout_f = grad_out.astype(jnp.float32)
    dy2_local = (valid_local * dout_f).astype(jnp.bfloat16)
    dy2 = lax.all_gather(dy2_local, "tensor", axis=0, tiled=True)
    up2 = trans_dot(dy2, b_lin2)
    dact = trans_dot(dy2, w_lin2) + ADAPT * exact_dot(up2, a_lin2.T)
    dpre = gelu_grad(dact)[0].astype(jnp.bfloat16)
    up1 = trans_dot(dpre, b_lin1)
    grad_lin2_up_t = ADAPT * cross_dot(down_2, dy2)
    grad_lin2_down_t = ADAPT * cross_dot(hidden_act, up2)
    grad_lin1_up_t = ADAPT * cross_dot(down_1, dpre)
    grad_lin1_down_t = ADAPT * cross_dot(xn2, up1)
    up_part = up1
    dxn2 = lax.psum_scatter(
        (trans_dot(dpre, w_lin1) + ADAPT * exact_dot(up_part, a_lin1.T)).astype(jnp.bfloat16),
        "tensor",
        scatter_dimension=0,
        tiled=True,
    ).astype(jnp.float32)
    dmiddle = dout_f + norm_back(dxn2, normal_two, inv_two, gain_two)
    dya_local = (valid_local * dmiddle).astype(jnp.bfloat16)
    dya = lax.all_gather(dya_local, "tensor", axis=0, tiled=True)
    upp = trans_dot(dya, b_proj)
    datt = (trans_dot(dya, proj_weight) + ADAPT * exact_dot(upp, a_proj.T)).astype(jnp.bfloat16)
    grad_proj_up_t = ADAPT * cross_dot(down_p, dya)
    grad_proj_down_t = ADAPT * cross_dot(att, upp)
    dqueries, dkeys, dvalues = attention_back(
        queries, key_win, value_win, log_total, to_windows(datt), table_h, table_w
    )
    dqkv = jnp.stack(
        [from_windows(dqueries), from_windows(dkeys), from_windows(dvalues)], axis=1
    ).reshape(full_rows, -1)
    upq = trans_dot(dqkv, b_qkv)
    grad_qkv_up_t = (ADAPT * cross_dot(down_q, dqkv)).reshape(RANK, 3, -1)
    grad_qkv_down_t = ADAPT * cross_dot(xn1, upq)
    up_part = upq
    dxn1 = lax.psum_scatter(
        (trans_dot(dqkv, qkv_flat) + ADAPT * exact_dot(up_part, a_qkv.T)).astype(jnp.bfloat16),
        "tensor",
        scatter_dimension=0,
        tiled=True,
    ).astype(jnp.float32)
    grad_tokens = (dmiddle + norm_back(valid_local * dxn1, normal_one, inv_one, gain_one)).astype(
        jnp.bfloat16
    )
    grad_qkv_up, grad_proj_down, grad_lin1_up, grad_lin2_down = lax.psum(
        (
            into_slot(grad_qkv_up_t),
            into_slot(grad_proj_down_t),
            into_slot(grad_lin1_up_t),
            into_slot(grad_lin2_down_t),
        ),
        "dp",
    )
    grad_qkv_down, grad_proj_up, grad_lin1_down, grad_lin2_up = lax.psum(
        (
            into_slot(grad_qkv_down_t),
            into_slot(grad_proj_up_t),
            into_slot(grad_lin1_down_t),
            into_slot(grad_lin2_up_t),
        ),
        ("dp", "tensor"),
    )
    return (
        output,
        grad_tokens,
        grad_qkv_down,
        grad_qkv_up,
        grad_proj_down,
        grad_proj_up,
        grad_lin1_down,
        grad_lin1_up,
        grad_lin2_down,
        grad_lin2_up,
    )


def solution(mesh):
    placed = (
        P(("dp", "tensor"), None),
        P(("dp", "tensor"), None),
        P(),
        P(),
        P(),
        P(None, None, "tensor"),
        P(None, "tensor"),
        P(),
        P(),
        P("tensor", None),
        P(),
        P(),
        P(),
        P(None, "tensor"),
        P("tensor"),
        P("tensor", None),
        P(),
        P(),
        P(None, None, None, "tensor"),
        P(None, "tensor", None),
        P(),
        P(),
        P(None, None, "tensor"),
        P(None, "tensor", None),
        P(),
    )
    return jax.shard_map(
        on_device,
        mesh=mesh,
        in_specs=placed,
        out_specs=(
            P(("dp", "tensor"), None),
            P(("dp", "tensor"), None),
            P(),
            P(None, None, None, "tensor"),
            P(None, "tensor", None),
            P(),
            P(),
            P(None, None, "tensor"),
            P(None, "tensor", None),
            P(),
        ),
        check_vma=False,
    )
```

profile of v0, /device:TPU:0, one launch (start us, length us, event | category | flops | bytes accessed | tf_op | source)
XLA Modules:
  0.0 929.5 jit_solution(8334608292282891529)
XLA Ops:
  19.2 28.9 %all-gather.9.cloned.1.call-done = bf16[4,343,1280]{2,1,0:T(8,128)(2,1)} async-done(((bf16[1,343,1280]{2,1,0:T(8,128)(2,1)}), bf16[4,343,1280]{2,1,0:T(8,128)(2,1)}) %all-gather.9.cloned.1.call-update) | async-done | bytes 3512336 | tf_op jit(solution)/shard_map/all_gather | solution.py:207
  48.1 4.7 reshape.204
  56.0 5.7 fusion.149
  68.7 3.9 reshape_squeeze.10
  72.6 3.8 copy.99
  78.8 3.9 reshape_squeeze.9
  85.0 3.9 reshape_squeeze.11
  88.9 3.8 copy.109
  96.2 3.9 copy.98
  100.1 6.8 convolution_bitcast_fusion.2
  106.9 5.8 copy.101
  112.7 6.8 convolution_bitcast_fusion.1
  119.5 6.3 copy.105
  125.8 16.1 %add.258 = f32[7,4,14,14,14,14]{5,4,3,2,1,0:T(8,128)} broadcast(f32[7,4,14,14,14]{4,3,2,1,0:T(8,128)} %copy.105), dimensions={0,1,2,3,5} | broadcast | bytes 4609920 | tf_op jit(solution)/shard_map/add | solution.py:88
  141.9 26.9 %add.259 = f32[7,4,196,196]{3,2,1,0:T(8,128)} reshape(f32[7,4,14,14,14,14]{5,4,3,2,1,0:T(8,128)} %add.258) | data formatting | bytes 8605184 | tf_op jit(solution)/shard_map/add | solution.py:88
  168.8 6.8 copy.106
  175.6 16.6 %add.255 = f32[7,4,14,14,14,14]{5,4,3,2,1,0:T(8,128)} broadcast(f32[7,4,14,14,14]{4,3,2,1,0:T(8,128)} %copy.101), dimensions={0,1,2,3,4} | broadcast | bytes 4609920 | tf_op jit(solution)/shard_map/add | solution.py:88
  192.2 26.9 %add.256 = f32[7,4,196,196]{3,2,1,0:T(8,128)} reshape(f32[7,4,14,14,14,14]{5,4,3,2,1,0:T(8,128)} %add.255) | data formatting | bytes 8605184 | tf_op jit(solution)/shard_map/add | solution.py:88
  219.1 6.5 copy.102
  225.5 6.3 fusion.148
  236.4 3.9 copy.110
  248.9 5.7 fusion.13
  254.6 35.5 %fusion = bf16[344,1280]{1,0:T(8,128)(2,1)} fusion(bf16[1372,1280]{1,0:T(8,128)(2,1)} %fusion.13), kind=kCustom, calls=%all-reduce-scatter | all-reduce-scatter fusion | flops 1761281 | bytes 4393472
  293.5 6.1 concatenate
  306.8 33.4 %all-gather.13.cloned.1.call-done = bf16[4,343,1280]{2,1,0:T(8,128)(2,1)} async-done(((bf16[1,343,1280]{2,1,0:T(8,128)(2,1)}), bf16[4,343,1280]{2,1,0:T(8,128)(2,1)}) %all-gather.13.cloned.1.call-update) | async-done | bytes 3512336 | tf_op jit(solution)/shard_map/all_gather | solution.py:273
  340.2 4.7 reshape.208
  348.1 9.0 fusion.152
  357.2 15.9 %all-gather.11.cloned.1.call-done = bf16[4,343,1280]{2,1,0:T(8,128)(2,1)} async-done(((bf16[1,343,1280]{2,1,0:T(8,128)(2,1)}), bf16[4,343,1280]{2,1,0:T(8,128)(2,1)}) %all-gather.11.cloned.1.call-update) | async-done | bytes 3512336 | tf_op jit(solution)/shard_map/all_gather | solution.py:244
  373.1 4.8 reshape.206
  381.1 4.9 convolution_add_fusion
  386.0 22.5 %multiply_convert_fusion = (bf16[1372,1280]{1,0:T(8,128)(2,1)}, f32[1372,1280]{1,0:T(8,128)S(1)}, f32[1372,1280]{1,0:T(8,128)}) fusion(f32[1372,1280]{1,0:T(8,128)S(1)} %convolution_add_fusion, f32[1372,16]{0,1:T(8,128)S(1)} %fusion.81, bf16[8,16,1280]{2,1,0:T(8,128)(2,1)} %param.47, s32[]{:T(128)S(6)} %select_n.86), kind=kOutput, calls=%fused_computation.21 | convolution fusion | flops 454845440 | bytes 24715012 | tf_op jit(solution)/shard_map/dot_general | solution.py:32
  408.5 9.7 %add_convert_fusion = bf16[1372,1280]{1,0:T(8,128)(2,1)S(1)} fusion(f32[1372,1280]{1,0:T(8,128)S(1)} %get-tuple-element.31, f32[1372,1280]{1,0:T(8,128)S(1)} %bitcast.198, f32[1372,16]{0,1:T(8,128)S(1)} %fusion.71, f32[1372,1280]{1,0:T(8,128)} %get-tuple-element.47, bf16[8,1280,16]{1,2,0:T(8,128)(2,1)} %param.48, s32[]{:T(128)S(6)} %select_n.86), kind=kOutput, calls=%fused_computation.20 | convolution fusion | flops 365281280 | bytes 24735492 | tf_op jit(solution)/shard_map/dot_general | solution.py:32
  420.0 4.8 fusion.153
  424.8 6.0 fusion.11
  430.9 35.2 %fusion.2 = bf16[344,1280]{1,0:T(8,128)(2,1)} fusion(bf16[1372,1280]{1,0:T(8,128)(2,1)} %fusion.11), kind=kCustom, calls=%all-reduce-scatter.2 | all-reduce-scatter fusion | flops 1761281 | bytes 4393472
  469.0 6.7 concatenate.2
  478.9 4.1 fusion.62
  497.3 4.8 fusion.151
  502.1 6.5 fusion.12
  508.5 9.3 all-gather.15.cloned.1.call-done
  517.8 4.7 reshape.210
  522.5 4.3 convolution_multiply_fusion.11
  536.2 3.9 reshape.194
  540.1 3.8 copy.112
  544.0 5.2 fusion.55
  549.1 4.3 multiply_reduce_fusion
  559.1 5.2 copy.117
  564.3 3.9 copy.128
  568.2 3.6 stack_reshape.11
  574.0 3.9 copy.125
  583.8 4.5 copy.116
  588.3 26.1 %reshape.202 = f32[7,4,14,14,14,14]{5,4,3,2,1,0:T(8,128)} reshape(f32[7,4,196,196]{3,2,1,0:T(8,128)} %copy.117) | data formatting | bytes 8605184 | tf_op jit(solution)/shard_map/reshape | solution.py:123
  614.4 19.9 %fusion.144 = (f32[7,4,14,14,14]{4,3,2,1,0:T(8,128)}, f32[7,4,14,14,14]{4,3,2,1,0:T(8,128)}) fusion(f32[7,4,14,14,14,14]{5,4,3,2,1,0:T(8,128)} %reshape.202), kind=kLoop, calls=%fused_computation.232 | loop fusion | flops 1997632 | bytes 4917248 | tf_op jit(solution)/shard_map/reduce_sum | solution.py:125
  634.3 4.4 fusion.23
  638.7 3.6 fusion.58
  644.1 3.6 stack_reshape.9
  666.6 6.4 convolution_bitcast_fusion
  673.0 5.7 fusion.10
  678.7 68.8 %fusion.145 = (bf16[344,1280]{1,0:T(8,128)(2,1)}, bf16[344,1280]{1,0:T(8,128)(2,1)}) fusion(bf16[1372,1280]{1,0:T(8,128)(2,1)} %fusion.12, bf16[1372,1280]{1,0:T(8,128)(2,1)} %fusion.10), kind=kCustom, calls=%all-reduce-scatter.4 | all-reduce-scatter fusion | flops 3522561 | bytes 8786432
  753.5 6.1 concatenate.3
  759.6 6.1 concatenate.1
  768.0 5.6 fusion.45
  773.5 31.3 %all-reduce.14.cloned.1.call-done = (f32[8,1280,16]{1,2,0:T(8,128)}, f32[8,16,1280]{2,1,0:T(8,128)}, f32[8,1280,16]{1,2,0:T(8,128)}, f32[8,16,1280]{2,1,0:T(8,128)}) async-done(((f32[8,1280,16]{1,2,0:T(8,128)}, f32[8,16,1280]{2,1,0:T(8,128)}, f32[8,1280,16]{1,2,0:T(8,128)}, f32[8,16,1280]{2,1,0:T(8,128)}), (f32[8,1280,16]{1,2,0:T(8,128)}, f32[8,16,1280]{2,1,0:T(8,128)}, f32[8,1280,16]{1,2,0:T(8,128)}, ...) | async-done | bytes 2621456 | tf_op jit(solution)/shard_map/psum | solution.py:324
  804.8 107.7 %all-reduce.16.cloned.1.call-done = (f32[8,16,3,320]{3,1,2,0:T(8,128)}, f32[8,320,16]{1,2,0:T(8,128)}, f32[8,16,1280]{2,1,0:T(8,128)}, f32[8,1280,16]{1,2,0:T(8,128)}) async-done(((f32[8,16,3,320]{3,1,2,0:T(8,128)}, f32[8,320,16]{1,2,0:T(8,128)}, f32[8,16,1280]{2,1,0:T(8,128)}, f32[8,1280,16]{1,2,0:T(8,128)}), (f32[8,16,3,320]{3,1,2,0:T(8,128)}, f32[8,320,16]{1,2,0:T(8,128)}, f32[8,16,1280]{2,1,0:T(8,128)}, ...) | async-done | bytes 1966096 | tf_op jit(solution)/shard_map/psum | solution.py:315
  (260 shorter events, 141.6 us)
Async XLA Ops:
  7.2 373.8 %copy-start = (bf16[1280,1280]{1,0:T(8,128)(2,1)S(1)}, bf16[1280,1280]{1,0:T(8,128)(2,1)}, u32[]{:S(2)}) copy-start(bf16[1280,1280]{1,0:T(8,128)(2,1)} %param.38) | copy-start | bytes 9830404
  7.2 7.4 copy-start.63
  7.2 9.3 %copy-start.58 = (bf16[3,320]{1,0:T(4,128)(2,1)S(1)}, bf16[3,320]{1,0:T(4,128)(2,1)}, u32[]{:S(2)}) copy-start(bf16[3,320]{1,0:T(4,128)(2,1)} %param.31) | copy-start | bytes 5764
  7.2 11.1 %copy-start.61 = (bf16[27,80]{1,0:T(8,128)(2,1)S(1)}, bf16[27,80]{1,0:T(8,128)(2,1)}, u32[]{:S(2)}) copy-start(bf16[27,80]{1,0:T(8,128)(2,1)} %param.33) | copy-start | bytes 12964
  7.2 11.5 %copy-start.62 = (bf16[27,80]{1,0:T(8,128)(2,1)S(1)}, bf16[27,80]{1,0:T(8,128)(2,1)}, u32[]{:S(2)}) copy-start(bf16[27,80]{1,0:T(8,128)(2,1)} %param.32) | copy-start | bytes 12964
  7.2 40.8 %all-gather.9.cloned.1.call-start = ((), (), s32[]{:S(2)}) async-start(), calls=%async_computation | async-start | bytes 4403200 | tf_op jit(solution)/shard_map/all_gather | solution.py:207
  8.8 8.6 copy-start.49
  10.4 7.0 copy-start.51
  11.1 6.3 copy-start.47
  14.5 325.7 %all-gather.13.cloned.1.call-start = ((), (), s32[]{:S(2)}) async-start(), calls=%async_computation.2 | async-start | bytes 4403200 | tf_op jit(solution)/shard_map/all_gather | solution.py:273
  18.3 43.4 %copy-start.45 = (bf16[16,960]{1,0:T(8,128)(2,1)}, bf16[16,960]{1,0:T(8,128)(2,1)S(1)}, u32[]{:S(2)}) copy-start(bf16[16,960]{1,0:T(8,128)(2,1)S(1)} %reshape.189) | copy-start | bytes 92164
  18.7 93.9 %copy-start.40 = (bf16[14,14,80,1,1]{2,1,0,3,4:T(8,128)(2,1)}, bf16[14,14,80,1,1]{2,1,0,3,4:T(8,128)(2,1)S(1)}, u32[]{:S(2)}) copy-start(bf16[14,14,80,1,1]{2,1,0,3,4:T(8,128)(2,1)S(1)} %reshape.212) | copy-start | bytes 94084
  19.2 80.9 %copy-start.42 = (bf16[14,14,80,1,1]{2,1,0,3,4:T(8,128)(2,1)}, bf16[14,14,80,1,1]{2,1,0,3,4:T(8,128)(2,1)S(1)}, u32[]{:S(2)}) copy-start(bf16[14,14,80,1,1]{2,1,0,3,4:T(8,128)(2,1)S(1)} %reshape.211) | copy-start | bytes 94084
  52.8 3.2 copy-start.4
  55.9 5.8 copy-start.27
  254.6 37.5 %copy-start.53 = (bf16[1280]{0:T(1024)(128)(2,1)S(1)}, bf16[1280]{0:T(1024)(128)(2,1)}, u32[]{:S(2)}) copy-start(bf16[1280]{0:T(1024)(128)(2,1)} %param.35) | copy-start | bytes 7684
  254.6 37.6 %copy-start.54 = (bf16[1280]{0:T(1024)(128)(2,1)S(1)}, bf16[1280]{0:T(1024)(128)(2,1)}, u32[]{:S(2)}) copy-start(bf16[1280]{0:T(1024)(128)(2,1)} %param.36) | copy-start | bytes 7684
  254.6 37.6 %copy-start.55 = (bf16[1280]{0:T(1024)(128)(2,1)S(1)}, bf16[1280]{0:T(1024)(128)(2,1)}, u32[]{:S(2)}) copy-start(bf16[1280]{0:T(1024)(128)(2,1)} %param.37) | copy-start | bytes 7684
  254.6 37.6 %copy-start.59 = (u32[32]{0:T(128)S(1)}, u32[32]{0:T(128)}, u32[]{:S(2)}) copy-start(u32[32]{0:T(128)} %constant.209) | copy-start | bytes 388
  290.8 2.6 collective-permute-start
  299.5 4.5 copy-start.2
  299.5 4.5 copy-start.12
  299.5 4.5 copy-start.26
  306.0 67.1 %all-gather.11.cloned.1.call-start = ((), (), s32[]{:S(2)}) async-start(), calls=%async_computation.1 | async-start | bytes 4403200 | tf_op jit(solution)/shard_map/all_gather | solution.py:244
  306.7 211.1 %all-gather.15.cloned.1.call-start = ((), (), s32[]{:S(2)}) async-start(), calls=%async_computation.3 | async-start | bytes 4403200 | tf_op jit(solution)/shard_map/all_gather | solution.py:291
  348.1 60.4 %copy-start.37 = (f32[1372,16]{0,1:T(8,128)}, f32[1372,16]{0,1:T(8,128)S(1)}, u32[]{:S(2)}) copy-start(f32[1372,16]{0,1:T(8,128)S(1)} %fusion.71) | copy-start | bytes 263428
  377.9 3.2 copy-start.6
  381.1 4.9 copy-start.38
  381.1 27.4 %slice-start.2 = ((s8[7045120]{0:T(1024)(128)(4,1)}), s8[4194304]{0:T(1024)(128)(4,1)S(1)}, s32[]{:S(2)}) async-start(s8[7045120]{0:T(1024)(128)(4,1)} %bitcast.197), calls=%async_computation.8 | async-start | bytes 8388608
  386.0 22.5 %slice-start.3 = ((s8[7045120]{0:T(1024)(128)(4,1)}), s8[2850816]{0:T(1024)(128)(4,1)S(1)}, s32[]{:S(2)}) async-start(s8[7045120]{0:T(1024)(128)(4,1)} %bitcast.197), calls=%async_computation.9 | async-start | bytes 5701632
  418.2 6.7 copy-start.15
  466.8 2.2 collective-permute-start.2
  475.7 3.2 copy-start.3
  475.7 3.2 copy-start.13
  475.7 3.2 copy-start.23
  483.1 321.8 %all-reduce.14.cloned.1.call-start = ((), (), s32[]{:S(2)}) async-start(), calls=%async_computation.4 | async-start | bytes 5242880 | tf_op jit(solution)/shard_map/psum | solution.py:324
  483.3 4.5 copy-start.14
  522.5 4.3 copy-start.11
  533.9 10.1 %copy-start.44 = (f32[7,4,196]{2,1,0:T(4,128)S(1)}, f32[7,4,196]{2,1,0:T(4,128)}, u32[]{:S(2)}) copy-start(f32[7,4,196]{2,1,0:T(4,128)} %log_add_fusion) | copy-start | bytes 65860
  544.0 5.2 copy-start.22
  544.0 5.2 copy-start.25
  544.0 9.5 %slice-start = ((s8[5734400]{0:T(1024)(128)(4,1)}), s8[4194304]{0:T(1024)(128)(4,1)S(1)}, s32[]{:S(2)}) async-start(s8[5734400]{0:T(1024)(128)(4,1)} %bitcast.182), calls=%async_computation.6 | async-start | bytes 8388608
  549.1 4.3 slice-start.1
  614.4 19.9 %copy-start.41 = (bf16[14,14,80,1,1]{2,1,0,3,4:T(8,128)(2,1)S(1)}, bf16[14,14,80,1,1]{2,1,0,3,4:T(8,128)(2,1)}, u32[]{:S(2)}) copy-start(bf16[14,14,80,1,1]{2,1,0,3,4:T(8,128)(2,1)} %copy-done.40) | copy-start | bytes 94084
  634.3 4.4 copy-start.18
  634.3 4.5 copy-start.19
  634.3 4.5 copy-start.43
  647.6 4.5 copy-start.28
  650.0 5.0 copy-start.46
  652.1 3.4 copy-start.5
  657.6 7.3 copy-start.35
  659.2 5.7 copy-start.36
  666.3 246.2 %all-reduce.16.cloned.1.call-start = ((), (), s32[]{:S(2)}) async-start(), calls=%async_computation.5 | async-start | bytes 4194304 | tf_op jit(solution)/shard_map/psum | solution.py:315
  678.7 74.8 %copy-start.57 = (bf16[1280]{0:T(1024)(128)(2,1)S(1)}, bf16[1280]{0:T(1024)(128)(2,1)}, u32[]{:S(2)}) copy-start(bf16[1280]{0:T(1024)(128)(2,1)} %param.41) | copy-start | bytes 7684
  747.5 18.1 %copy-start.48 = (f32[1280]{0:T(1024)S(1)}, f32[1280]{0:T(1024)}, u32[]{:S(2)}) copy-start(f32[1280]{0:T(1024)} %copy-done.47) | copy-start | bytes 15364
  747.5 18.1 %copy-start.50 = (f32[343]{0:T(512)S(1)}, f32[343]{0:T(512)}, u32[]{:S(2)}) copy-start(f32[343]{0:T(512)} %copy-done.49) | copy-start | bytes 4120
  747.5 18.1 %copy-start.52 = (f32[343]{0:T(512)S(1)}, f32[343]{0:T(512)}, u32[]{:S(2)}) copy-start(f32[343]{0:T(512)} %copy-done.51) | copy-start | bytes 4120
  748.3 5.2 collective-permute-start.3
  750.3 9.2 collective-permute-start.1
  912.5 5.7 copy-start.32
  912.5 6.6 copy-start.31
  912.5 7.4 copy-start.34
  912.5 8.2 copy-start.33
  914.7 7.0 copy-start.30
  (14 other events, 31.9 us)
Sparse Core Ops, SparseCore 0:
  14.7 33.3 all-gather.8
  306.1 34.0 all-gather.12
  342.4 30.6 all-gather.10
  483.2 34.5 all-gather.14
  666.4 138.3 all-reduce.13
  810.3 102.1 all-reduce.15
where the time goes:
time: 941 us; the launch traced here: 930 us
  local copies, waits for them, and re-layouts  291 us (31%)
  waiting for transfers between devices  228 us (24%)
  matrix products  184 us (20%)
  blocking collectives  140 us (15%)
  other arithmetic  61.4 us (7%)
  between operations  17.9 us (2%)
    unnamed x3, blocking collectives  140 us
    psum x1, waiting for transfers between devices, on_device(): lax.psum((into_slot(grad_qkv_up_t), into_slot(grad_proj_down_t), into_slo...  108 us
    add x6, local copies, waits for them, and re-layouts, window_scores(): base_scores.reshape(win_count, head_count, WIN, WIN, WIN, WIN)  99.8 us
    unnamed x160, local copies, waits for them, and re-layouts  66.6 us
    dot_general x10, matrix products, exact_dot(): return jnp.dot(first_op, second_op.astype(jnp.float32), precision=HIGH)  62.1 us
    all_gather x1, waiting for transfers between devices, on_device(): dy2 = lax.all_gather(dy2_local, 'tensor', axis=0, tiled=True)  33.4 us
    reshape x2, local copies, waits for them, and re-layouts, attention_back(): dscore.astype(jnp.float32)  31.3 us
    psum x1, waiting for transfers between devices, on_device(): lax.psum((into_slot(grad_qkv_down_t), into_slot(grad_proj_up_t), into_slo...  31.3 us
  transfers between devices with their start and end apart: 10, of which 7 were waited for; matrix products, arithmetic and copies ran while one was open for 16% of the time, Pallas kernels for 0%

commit v1 on v0

v1 whole, which is shorter than its diff:
```python
import functools

import jax
import jax.numpy as jnp
import numpy as np
from jax import lax
from jax.experimental import pallas as pl
from jax.experimental.pallas import tpu as pltpu
from jax.sharding import PartitionSpec as P

HEAD_DIM = 80
WIN = 14
SIDE = 64
RANK = 16
ADAPTERS = 8
WIN_DEV = 7
GROUP = 4
GRID = 5
TOK = WIN * WIN
PAD = 208
NW = 2
R = NW * PAD
D = 1280
LOC = 320
LP = 384
HID = 1280
HC = 256
PACK = 3584
EXT = 32
HALF = 0.5
EPS = 1e-6
SCALE = HEAD_DIM**-0.5
MESH = pl.DeviceIdType.MESH
BF = jnp.bfloat16
F32 = jnp.float32
SPAN = ((0, 128), (0, 256), (128, 128), (128, 256))
ERF_P = 0.3275911
ERF_A = (0.254829592, -0.284496736, 1.421413741, -1.453152027, 1.061405429)

CHUNKS = (
    [("q", 0, 320), ("q", 320, 320), ("q", 640, 320), ("p", 0, 320)]
    + [("1", 320 * i, 320) for i in range(4)]
    + [("2", 256 * i, 256) for i in range(5)]
)
NCH = len(CHUNKS)
THIRDS = {80: ((2, 2, 1), (2, 1, 2), (1, 2, 2)), 64: ((2, 1, 1), (1, 2, 1), (1, 1, 2))}


def nn(a, b):
    return jnp.dot(a, b, preferred_element_type=F32)


def nt(a, b):
    return lax.dot_general(a, b, (((1,), (1,)), ((), ())), preferred_element_type=F32)


def tn(a, b):
    return lax.dot_general(a, b, (((0,), (0,)), ((), ())), preferred_element_type=F32)


def mult(v, m=16):
    return v if isinstance(v, int) else pl.multiple_of(v, m)


class Wire:
    def __init__(self, own, land, pack_own, pack_land, sems):
        self.own, self.land, self.sems = own, land, sems
        self.pack_own, self.pack_land = pack_own, pack_land
        dp, t = lax.axis_index("dp"), lax.axis_index("tensor")
        self.q = lax.rem(dp, 4)
        self.dev = {"x": (dp ^ 1, t), "z": (dp ^ 2, t), "y": (dp, t ^ 2), "c": (dp, t ^ 1)}
        self.count = {}

    def barrier(self):
        bar = pltpu.get_barrier_semaphore()
        for d in self.dev.values():
            pl.semaphore_signal(bar, inc=1, device_id=d, device_id_type=MESH)
        pl.semaphore_wait(bar, len(self.dev))

    def copy(self, key, src, dst, dev):
        n = self.count.setdefault(key, len(self.count))
        return pltpu.make_async_remote_copy(
            src_ref=src,
            dst_ref=dst,
            send_sem=self.sems.at[0, n],
            recv_sem=self.sems.at[1, n],
            device_id=self.dev[dev],
            device_id_type=MESH,
        )

    def pack(self, what):
        return {
            "c": lambda: self.copy("pc", self.pack_own, self.pack_land.at[1], "c"),
            "y": lambda: self.copy("py", self.pack_own, self.pack_land.at[2], "y"),
            "f": lambda: self.copy("pf", self.pack_land.at[2], self.pack_land.at[3], "c"),
        }[what]()

    def parts(self, c):
        name, first, rows = CHUNKS[c]
        quarter = rows // 4
        a, b, d = (16 * v for v in THIRDS[quarter][c % 3])
        q = self.q

        def at(quart, off, n):
            return pl.ds(mult(first + quart * quarter + off), n)

        return {
            "y1": at(q, 0, quarter),
            "y2": at(q ^ 3, 0, a),
            "x1": at(q ^ 1, 0, quarter),
            "z1": at(q ^ 2, 0, quarter),
            "d": at(q ^ 3, a, b + d),
            "xs": at(q, 0, quarter),
            "x2": at(q ^ 2, a, b),
            "z2": at(q ^ 1, a + b, d),
        }

    def piece(self, c, what):
        name, first, rows = CHUNKS[c]
        own, land = self.own[name], self.land[name]
        p = self.parts(c)
        if what == "s":
            s = pl.ds(first, rows)
            return self.copy((c, what), own.at[s], land.at[1, s], "c")
        if what in ("y1", "y2"):
            return self.copy((c, what), own.at[p[what]], land.at[2, p[what]], "y")
        if what in ("x1", "z1"):
            return self.copy((c, what), land.at[2, p["xs"]], land.at[2, p["xs"]], what[0])
        if what in ("x2", "z2"):
            return self.copy((c, what), land.at[2, p[what]], land.at[2, p[what]], what[0])
        r = p[what[1:]]
        return self.copy((c, what), land.at[2, r], land.at[3, r], "c")

    def begin(self):
        self.pack("c").start()
        self.pack("y").start()
        for c in range(NCH):
            self.piece(c, "y1").start()
            self.piece(c, "y2").start()
            self.piece(c, "s").start()

    def step(self, n):
        if n == 0:
            self.pack("y").wait_recv()
            self.pack("f").start()
        if n < NCH:
            for w in ("y1", "y2"):
                self.piece(n, w).wait_recv()
            for w in ("x1", "z1", "cy1", "cy2"):
                self.piece(n, w).start()
        if 0 <= n - 1 < NCH:
            for w in ("x1", "z1"):
                self.piece(n - 1, w).wait_recv()
            for w in ("x2", "z2", "cx1", "cz1"):
                self.piece(n - 1, w).start()
        if 0 <= n - 2 < NCH:
            for w in ("x2", "z2"):
                self.piece(n - 2, w).wait_recv()
            self.piece(n - 2, "cd").start()

    def have(self, k, chunks):
        for c in chunks:
            if k == 1:
                self.piece(c, "s").wait_recv()
            if k == 3:
                for w in ("cy1", "cy2", "cx1", "cz1", "cd"):
                    self.piece(c, w).wait_recv()

    def finish(self):
        for w in "cyf":
            self.pack(w).wait_send()
        for c in range(NCH):
            for w in ("s", "y1", "y2", "x1", "z1", "x2", "z2", "cy1", "cy2", "cx1", "cz1", "cd"):
                self.piece(c, w).wait_send()


STEPS = NCH + 2


def shifted(values, shift, right):
    for bit in (1, 2, 4, 8):
        moved = pltpu.roll(values, bit if right else 128 - bit, 1)
        values = jnp.where((shift & bit) > 0, moved, values)
    return values


def join_heads(parts):
    lane = lax.broadcasted_iota(jnp.int32, (PAD, 128), 1)
    t0 = jnp.where(lane < 80, parts[0], parts[1][:, :128])
    t1 = jnp.where(
        lane < 32, parts[1][:, 128:], jnp.where(lane < 112, parts[2], parts[3][:, :128])
    )
    return (t0, t1, parts[3][:, 128:])


def head_mask(h, dtype=BF):
    base, width = SPAN[h]
    low = HEAD_DIM * h - base
    lane = lax.broadcasted_iota(jnp.int32, (1, width), 1)
    return jnp.where((lane >= low) & (lane < low + HEAD_DIM), 1.0, 0.0).astype(dtype)


def stats(v):
    mean = jnp.mean(v, axis=-1, keepdims=True)
    cen = v - mean
    inv = lax.rsqrt(jnp.mean(cen * cen, axis=-1, keepdims=True) + EPS)
    return cen * inv, inv


def norm_back(grad, xhat, inv, gain):
    e = grad * gain
    return inv * (
        e
        - jnp.mean(e, axis=-1, keepdims=True)
        - xhat * jnp.mean(e * xhat, axis=-1, keepdims=True)
    )


def row_loop(body, rows=32):
    def one(i, _):
        body(pl.ds(mult(i * rows, 32), rows))
        return 0

    lax.fori_loop(0, R // rows, one, 0)


def ticks(wire, place, index):
    for n, at in place.items():

        @pl.when(index == at)
        def _():
            wire.step(n)


def kernel(
    x_hbm, g_hbm, wq_hbm, wp_hbm, w1_hbm, w2_hbm, pack_hbm,
    vec_ref, adp_ref, valid_ref, shift_ref, rel_ref, hot_ref, back_ref, key_ref,
    out_hbm, grad_hbm, g_rep, g_bq, g_ap, g_b1, g_a2,
    x_s, g_s, wq, wp, w1, w2, pack, xn_s, q_s, k_s, v_s, att_s, p_s, mid_s, acc_a, acc_b,
    datt_s, d1t_s, up2t_s, d1_s, up2_s, d2_s, up1_s, upq_s, dqt_s, sems, local,
):
    own = {"q": wq_hbm, "p": wp_hbm, "1": w1_hbm, "2": w2_hbm}
    land = {"q": wq, "p": wp, "1": w1, "2": w2}
    wire = Wire(own, land, pack_hbm, pack, sems)
    wire.barrier()
    wire.begin()
    pairs = [
        (x_hbm, x_s), (pack_hbm, pack.at[0]), (wq_hbm, wq.at[0]), (wp_hbm, wp.at[0]),
        (g_hbm, g_s), (w1_hbm, w1.at[0]), (w2_hbm, w2.at[0]),
    ]
    loads = [pltpu.make_async_copy(a, b, local.at[i]) for i, (a, b) in enumerate(pairs)]
    for cp in loads:
        cp.start()
    lane_pad = jnp.zeros((4, R, LP - 256), BF)
    for ref in (q_s, k_s, v_s, att_s):
        ref[:, :, 256:LP] = lane_pad
    datt_s[:, 256:LP] = lane_pad[0]

    gain1, shift1, gain2, shift2 = (vec_ref[i : i + 1, :] for i in range(4))
    bias_p, bias_2 = vec_ref[4:5, :], vec_ref[5:6, :]
    a_q, a_1, b_p, b_2 = (adp_ref[i] for i in range(4))
    lane_e = lax.broadcasted_iota(jnp.int32, (R, EXT), 1)
    valid = valid_ref[...]

    loads[0].wait()

    def norm_one(rows):
        xhat, _ = stats(x_s[rows, :].astype(F32))
        xn_s[rows, :] = (valid_ref[rows, :] * (xhat * gain1 + shift1)).astype(BF)

    row_loop(norm_one)
    loads[1].wait()
    down_q = HALF * nt(xn_s[...], a_q)
    dq_ext = jnp.where(lane_e == RANK, 1.0, down_q).astype(BF)
    d1_s[...] = dq_ext
    dqt_s[...] = down_q.T.astype(BF)
    loads[2].wait()

    def heads_forward(k, _):
        @pl.when(k == 1)
        def _():
            wire.pack("c").wait_recv()
            wire.have(1, range(3))

        @pl.when(k == 2)
        def _():
            for n in range(5):
                wire.step(n)

        @pl.when(k == 3)
        def _():
            wire.pack("f").wait_recv()
            wire.have(3, range(3))

        qkv = nt(xn_s[...], wq[k]) + nn(d1_s[...], pack[k, :, 0 : 3 * LOC])
        q_s[k, :, 0:LOC] = qkv[:, 0:LOC].astype(BF)
        k_s[k, :, 0:LOC] = qkv[:, LOC : 2 * LOC].astype(BF)
        v_s[k, :, 0:LOC] = qkv[:, 2 * LOC : 3 * LOC].astype(BF)

        def window(w, _):
            rows = pl.ds(mult(w * PAD), PAD)
            shift = shift_ref[...]
            lane = lax.broadcasted_iota(jnp.int32, (PAD, 128), 1)
            fine = (lane & 32) > 0
            outs = []
            for h in range(4):
                b, n = SPAN[h]
                lanes = slice(b, b + n)
                qm = q_s[k, rows, lanes] * head_mask(h)
                scores = nt(qm, k_s[k, rows, lanes]) * SCALE
                u = shifted(nt(qm, rel_ref[h, :, lanes]), shift, False)
                rest = u - u.astype(BF).astype(F32)
                u = jnp.where(fine, pltpu.roll(rest, 32, 1), u).astype(BF)
                scores = scores + nn(u, hot_ref[...]) + key_ref[...]
                top = jnp.max(scores, axis=1, keepdims=True)
                e = jnp.exp(scores - top)
                p = (e * (1.0 / jnp.sum(e, axis=1, keepdims=True))).astype(BF)
                p_s[(k * NW + w) * 4 + h] = p
                outs.append(nn(p, v_s[k, rows, lanes]))
            for i, part in enumerate(join_heads(outs)):
                att_s[k, rows, 128 * i : 128 * i + 128] = part.astype(BF)
            return 0

        lax.fori_loop(0, NW, window, 0)
        return 0

    lax.fori_loop(0, 4, heads_forward, 0)

    loads[3].wait()
    wire.have(1, [3])
    wire.step(5)
    wire.have(3, [3])
    down_p = jnp.zeros((R, RANK), F32)
    for k in range(4):
        down_p += nt(att_s[k, :, 0:LOC], pack[k, 16:32, 2304 : 2304 + LOC])
    down_p = HALF * down_p
    dp16 = down_p.astype(BF)
    dpt = down_p.T.astype(BF)
    for n in range(5):
        cols = slice(256 * n, 256 * n + 256)
        total = nn(dp16, b_p[:RANK, cols]) + bias_p[:, cols]
        for k in range(4):
            total += nn(att_s[k, :, 0:LOC], wp[k, :, cols])
        acc_a[:, cols] = total

    def norm_two(rows):
        mid = x_s[rows, :].astype(F32) + valid_ref[rows, :] * acc_a[rows, :]
        mid_s[rows, :] = mid
        xhat, _ = stats(mid)
        xn_s[rows, :] = (xhat * gain2 + shift2).astype(BF)

    row_loop(norm_two)
    down_1 = HALF * nt(xn_s[...], a_1)
    d1_s[...] = jnp.where(lane_e == RANK, 1.0, down_1).astype(BF)
    d1t_s[...] = down_1.T.astype(BF)
    loads[4].wait()
    up2 = HALF * valid * nt(g_s[...], b_2)
    up2_s[...] = up2.astype(BF)
    up2t_s[...] = up2.T.astype(BF)
    acc_a[...] = jnp.zeros((R, D), F32)
    acc_b[...] = jnp.zeros((R, D), F32)
    d2_s[...] = jnp.zeros((R, EXT), F32)
    up1_s[...] = jnp.zeros((R, EXT), F32)
    loads[5].wait()
    loads[6].wait()

    def hidden(i, _):
        late = i - 10
        k = jnp.where(i < 5, 0, jnp.where(i < 10, 1, 2 + lax.rem(late + 10, 2)))
        c = jnp.where(i < 10, lax.rem(i, 5), (late + 10) // 2 - 5)

        @pl.when(i == 5)
        def _():
            wire.have(1, range(4, NCH))

        ticks(wire, {6: 2, 7: 6, 8: 9, 9: 10, 10: 10, 11: 12, 12: 14, 13: 16, 14: 18}, i)

        @pl.when(i == 11)
        def _():
            wire.have(3, range(4, 8))

        for j in range(5):

            @pl.when(i == 11 + 2 * j)
            def _():
                wire.have(3, [8 + j])

        cols = pl.ds(mult(c * HC, HC), HC)
        pcols = pl.ds(mult(1024 + c * HC, HC), HC)
        acols = pl.ds(mult(2304 + c * HC, HC), HC)
        pre = nn(xn_s[...], w1[k, :, cols]) + nn(d1_s[...], pack[k, :, pcols])
        gauss = jnp.exp(-0.5 * pre * pre)
        t = 1.0 / (1.0 + (ERF_P * 0.5**0.5) * jnp.abs(pre))
        poly = ERF_A[4]
        for a in ERF_A[3::-1]:
            poly = poly * t + a
        tail = (HALF * poly) * t * gauss
        phi = jnp.where(pre >= 0, 1.0 - tail, tail)
        act = (pre * phi).astype(BF)
        slope = phi + pre * gauss * 0.3989422804014327
        a2 = pack[k, :, acols]
        g_a2[k, :, cols] = nn(up2t_s[...], act)[:RANK]
        d2_s[...] += nt(act, a2)
        dact = valid * nt(g_s[...], w2[k, cols, :]) + nn(up2_s[...], a2)
        dpre = (dact * slope).astype(BF)
        g_b1[k, :, cols] = nn(d1t_s[...], dpre)[:RANK]
        up1_s[...] += nt(dpre, pack[k, :, pcols])
        for n in range(5):
            out = slice(256 * n, 256 * n + 256)
            acc_a[:, out] += nn(act, w2[k, cols, out])
            acc_b[:, out] += nt(dpre, w1[k, out, cols])
        return 0

    lax.fori_loop(0, 20, hidden, 0)

    d2 = HALF * d2_s[...]
    d2b = d2.astype(BF)
    up1 = HALF * up1_s[...]
    up1b = up1.astype(BF)
    g_rep[3] = nn((d2 * valid).T.astype(BF), g_s[...])[:RANK]
    g_rep[2] = nn(up1.T.astype(BF), xn_s[...])[:RANK]
    for n in range(5):
        cols = slice(256 * n, 256 * n + 256)
        acc_a[:, cols] += nn(d2b, b_2[:, cols])
        acc_b[:, cols] += nn(up1b, a_1[:, cols])

    def back_two(rows):
        mid = mid_s[rows, :]
        ok = valid_ref[rows, :]
        x_out = mid + ok * (acc_a[rows, :] + bias_2)
        xhat, inv = stats(mid)
        dmid = g_s[rows, :].astype(F32) + norm_back(acc_b[rows, :], xhat, inv, gain2)
        mid_s[rows, :] = dmid
        g_s[rows, :] = (ok * dmid).astype(BF)
        xn_s[rows, :] = x_out.astype(BF)

    row_loop(back_two)
    put_out = pltpu.make_async_copy(xn_s, out_hbm, local.at[7])
    put_out.start()
    upp = HALF * nt(g_s[...], b_p)
    upp16 = upp[:, :RANK].astype(BF)
    uppt = upp.T.astype(BF)
    g_rep[1] = nn(dpt, g_s[...])
    acc_a[...] = jnp.zeros((R, D), F32)
    upq_s[...] = jnp.zeros((R, EXT), F32)
    up2_s[:, 0:RANK] = upp16
    up2t_s[...] = uppt

    def heads_backward(k, _):
        datt = nt(g_s[...], wp[k]) + nn(up2_s[:, 0:RANK], pack[k, 16:32, 2304 : 2304 + LOC])
        datt_s[:, 0:LOC] = datt.astype(BF)
        g_ap[k] = nn(up2t_s[...], att_s[k, :, 0:LOC])[:RANK]

        def window(w, _):
            rows = pl.ds(mult(w * PAD), PAD)
            shift = shift_ref[...]
            dqs, dks, dvs = [], [], []
            for h in range(4):
                b, n = SPAN[h]
                lanes = slice(b, b + n)
                p = p_s[(k * NW + w) * 4 + h]
                da = datt_s[rows, lanes]
                dprob = nt(da * head_mask(h), v_s[k, rows, lanes])
                dvs.append(tn(p, da))
                pf = p.astype(F32)
                inner = jnp.sum(pf * dprob, axis=1, keepdims=True)
                ds = (pf * (dprob - inner)).astype(BF)
                du = shifted(nn(ds, back_ref[...]), shift, True).astype(BF)
                dqs.append(nn(ds, k_s[k, rows, lanes]) * SCALE + nn(du, rel_ref[h, :, lanes]))
                dks.append(tn(ds, q_s[k, rows, lanes]) * SCALE)
            for ref, parts in ((q_s, dqs), (k_s, dks), (v_s, dvs)):
                for i, part in enumerate(join_heads(parts)):
                    ref[k, rows, 128 * i : 128 * i + 128] = part.astype(BF)
            return 0

        lax.fori_loop(0, NW, window, 0)
        for j, ref in enumerate((q_s, k_s, v_s)):
            d = ref[k, :, 0:LOC]
            b = pack[k, :, j * LOC : (j + 1) * LOC]
            upq_s[...] += nt(d, b)
            g_bq[k, j] = nn(dqt_s[...], d)[:RANK]
        for n in range(5):
            cols = slice(256 * n, 256 * n + 256)
            total = acc_a[:, cols]
            for j, ref in enumerate((q_s, k_s, v_s)):
                total += nn(ref[k, :, 0:LOC], wq[k, j * LOC : (j + 1) * LOC, cols])
            acc_a[:, cols] = total
        return 0

    lax.fori_loop(0, 4, heads_backward, 0)
    put_out.wait()

    upq = HALF * upq_s[...]
    upqb = upq.astype(BF)
    upqt = upq.T.astype(BF)
    for n in range(5):
        cols = slice(256 * n, 256 * n + 256)
        acc_a[:, cols] += nn(upqb, a_q[:, cols])

    def back_one(rows):
        ok = valid_ref[rows, :]
        xhat, inv = stats(x_s[rows, :].astype(F32))
        xn_s[rows, :] = (ok * (xhat * gain1 + shift1)).astype(BF)
        back = norm_back(ok * acc_a[rows, :], xhat, inv, gain1)
        g_s[rows, :] = (mid_s[rows, :] + back).astype(BF)

    row_loop(back_one)
    put_grad = pltpu.make_async_copy(g_s, grad_hbm, local.at[8])
    put_grad.start()
    g_rep[0] = nn(upqt, xn_s[...])[:RANK]
    put_grad.wait()
    wire.finish()


def tables(rel_pos_h, rel_pos_w):
    flip = np.zeros((2, 128, 2 * WIN - 1), np.float32)
    for i in range(2 * WIN - 1):
        flip[0, i, 2 * WIN - 2 - i] = 1
        flip[1, 64 + i, 2 * WIN - 2 - i] = 1
    rel = jnp.dot(flip[0].astype(BF), rel_pos_h) + jnp.dot(flip[1].astype(BF), rel_pos_w)
    zero = lambda n: jnp.zeros((128, n), BF)
    rel = jnp.stack(
        [
            jnp.concatenate([zero(80 * h), rel, zero(LP - 80 * h - 80)], axis=1)
            for h in range(LOC // HEAD_DIM)
        ]
    )
    tok = np.arange(PAD)
    inside = tok < TOK
    row, col = tok // WIN, tok % WIN
    lane = np.arange(128)[:, None]
    hot = (
        (((lane == row) | (lane == 32 + row)) & inside)
        | (((lane == 64 + col) | (lane == 96 + col)) & inside)
    ).astype(np.float32)
    back = ((lane == row) | (lane == 64 + col)) & inside
    shift = np.where(np.arange(128)[None] < 64, 13 - row[:, None], 13 - col[:, None])
    shift = np.where(inside[:, None], shift, 0).astype(np.int32)
    key = np.where(inside, 0.0, -1e30).astype(np.float32)[None]
    return rel, jnp.asarray(hot, BF), jnp.asarray(back.T, BF), jnp.asarray(shift), jnp.asarray(key)


def call_kernel(args):
    any_ = pl.BlockSpec(memory_space=pl.ANY)
    vmem = pl.BlockSpec(memory_space=pltpu.VMEM)
    sds = jax.ShapeDtypeStruct
    V = pltpu.VMEM
    return pl.pallas_call(
        kernel,
        out_shape=(
            sds((R, D), BF),
            sds((R, D), BF),
            sds((4, RANK, D), F32),
            sds((4, 3, RANK, LOC), F32),
            sds((4, RANK, LOC), F32),
            sds((4, RANK, HID), F32),
            sds((4, RANK, HID), F32),
        ),
        in_specs=[any_] * 7 + [vmem] * 8,
        out_specs=(any_, any_) + (vmem,) * 5,
        scratch_shapes=[
            V((R, D), BF),
            V((R, D), BF),
            V((4, 3 * LOC, D), BF),
            V((4, LOC, D), BF),
            V((4, D, HID), BF),
            V((4, HID, D), BF),
            V((4, EXT, PACK), BF),
            V((R, D), BF),
            V((4, R, LP), BF),
            V((4, R, LP), BF),
            V((4, R, LP), BF),
            V((4, R, LP), BF),
            V((4 * NW * 4, PAD, PAD), BF),
            V((R, D), F32),
            V((R, D), F32),
            V((R, D), F32),
            V((R, LP), BF),
            V((EXT, R), BF),
            V((EXT, R), BF),
            V((R, EXT), BF),
            V((R, EXT), BF),
            V((R, EXT), F32),
            V((R, EXT), F32),
            V((R, EXT), F32),
            V((EXT, R), BF),
            pltpu.SemaphoreType.DMA((2, 12 * NCH + 3)),
            pltpu.SemaphoreType.DMA((9,)),
        ],
        compiler_params=pltpu.CompilerParams(
            collective_id=0, has_side_effects=True, vmem_limit_bytes=66_500_000
        ),
        name="block",
    )(*args)


def on_device(
    tokens,
    grad_out,
    adapter_index,
    norm1_gain,
    norm1_shift,
    qkv_weight,
    qkv_bias,
    rel_pos_h,
    rel_pos_w,
    proj_weight,
    proj_bias,
    norm2_gain,
    norm2_shift,
    lin1_weight,
    lin1_bias,
    lin2_weight,
    lin2_bias,
    qkv_down,
    qkv_up,
    proj_down,
    proj_up,
    lin1_down,
    lin1_up,
    lin2_down,
    lin2_up,
):
    tensor_size = lax.axis_size("tensor")
    images = adapter_index.shape[0]
    row_count = tokens.shape[0]
    t = lax.axis_index("tensor")
    dp_place = lax.axis_index("dp")
    image = dp_place // GROUP
    pick = jnp.sum(jnp.where(jnp.arange(images) == image, adapter_index, 0))

    def select(table_all):
        return lax.dynamic_index_in_dim(table_all, pick, 0, keepdims=False)

    work = NW * TOK
    gap = work - row_count
    far = gap * (tensor_size - 1)
    both = jnp.stack([tokens, grad_out])
    more = lax.ppermute(both[:, :far], "tensor", [(s, s - 1) for s in range(1, tensor_size)])
    none = jnp.zeros((2, gap, D), BF)
    both = lax.dynamic_slice_in_dim(jnp.concatenate([both, more, none], axis=1), gap * t, work, 1)
    both = jnp.pad(both.reshape(2, NW, TOK, D), ((0, 0), (0, 0), (0, PAD - TOK), (0, 0)))
    x, g = both.reshape(2, R, D)

    place = jnp.arange(R, dtype=jnp.int32)
    window = place // PAD + NW * t
    slot = dp_place % GROUP * WIN_DEV + window
    within = place % PAD
    image_row = slot // GRID * WIN + within // WIN
    image_col = slot % GRID * WIN + within % WIN
    valid = (within < TOK) & (window < WIN_DEV) & (slot < GRID * GRID)
    valid = valid & (image_row < SIDE) & (image_col < SIDE)
    valid = jnp.where(valid, 1.0, 0.0).astype(F32)[:, None]

    wq = jnp.transpose(qkv_weight, (1, 2, 0)).reshape(3 * LOC, D)
    row = lambda v: v.reshape(1, -1)
    bq = jnp.transpose(select(qkv_up), (0, 1, 2)).reshape(RANK, 3 * LOC)
    pad_rows = lambda v, n: jnp.pad(v, ((0, n - v.shape[0]), (0, 0)))
    bq = pad_rows(jnp.concatenate([bq, row(qkv_bias)]), EXT)
    b1 = pad_rows(jnp.concatenate([select(lin1_up), row(lin1_bias)]), EXT)
    low = jnp.concatenate(
        [select(lin2_down).T, jnp.pad(select(proj_down).T, ((0, 0), (0, HID - LOC)))]
    )
    pack = jnp.concatenate([bq, jnp.zeros((EXT, 1024 - 3 * LOC), BF), b1, low], axis=1)
    vecs = jnp.stack([norm1_gain, norm1_shift, norm2_gain, norm2_shift, proj_bias, lin2_bias])
    vecs = jnp.pad(vecs.astype(F32), ((0, 2), (0, 0)))
    adps = jnp.stack([select(qkv_down).T, select(lin1_down).T, select(proj_up), select(lin2_up)])
    adps = jnp.pad(adps, ((0, 0), (0, EXT - RANK), (0, 0)))
    rel, hot, back, shift, key = tables(rel_pos_h, rel_pos_w)
    out, grad, g_rep, g_bq, g_ap, g_b1, g_a2 = call_kernel(
        (x, g, wq, proj_weight, lin1_weight, lin2_weight, pack,
         vecs, adps, valid, shift, rel, hot, back, key)
    )

    ends = jnp.stack([out, grad]).reshape(2, NW, PAD, D)[:, :, :TOK].reshape(2, work, D)
    more = lax.ppermute(
        ends[:, work - far :], "tensor", [(s, s + 1) for s in range(tensor_size - 1)]
    )
    ends = jnp.concatenate([more, ends], axis=1)
    output, grad_tokens = lax.dynamic_slice_in_dim(ends, far - gap * t, row_count, 1)

    order = t ^ jnp.arange(tensor_size)
    split = jnp.concatenate(
        [v.reshape(tensor_size, -1) for v in (g_bq, g_ap, g_b1, g_a2)], axis=1
    )
    split = lax.psum_scatter(split[order], "tensor", scatter_dimension=0, tiled=False)
    mine = jnp.where(jnp.arange(images) == image, 1.0, 0.0).astype(F32)
    split = lax.psum(mine[:, None] * split[None], "dp")
    whole = lax.psum(mine[:, None, None, None] * g_rep[None], ("dp", "tensor"))
    slots = jnp.where(
        jnp.arange(ADAPTERS)[:, None] == adapter_index[None], 1.0, 0.0
    ).astype(F32)
    to_slots = lambda v: jnp.einsum("ai,i...->a...", slots, v, precision=lax.Precision.HIGHEST)
    split, whole = to_slots(split), to_slots(whole)
    sizes = np.cumsum([3 * RANK * LOC, RANK * LOC, RANK * HID])
    s_bq, s_ap, s_b1, s_a2 = jnp.split(split, sizes, axis=1)
    swap = lambda v: jnp.swapaxes(v, 1, 2)
    return (
        output,
        grad_tokens,
        swap(whole[:, 0]),
        jnp.swapaxes(s_bq.reshape(ADAPTERS, 3, RANK, LOC), 1, 2),
        swap(s_ap.reshape(ADAPTERS, RANK, LOC)),
        whole[:, 1],
        swap(whole[:, 2]),
        s_b1.reshape(ADAPTERS, RANK, HID),
        swap(s_a2.reshape(ADAPTERS, RANK, HID)),
        whole[:, 3],
    )


def solution(mesh):
    placed = (
        P(("dp", "tensor"), None),
        P(("dp", "tensor"), None),
        P(),
        P(),
        P(),
        P(None, None, "tensor"),
        P(None, "tensor"),
        P(),
        P(),
        P("tensor", None),
        P(),
        P(),
        P(),
        P(None, "tensor"),
        P("tensor"),
        P("tensor", None),
        P(),
        P(),
        P(None, None, None, "tensor"),
        P(None, "tensor", None),
        P(),
        P(),
        P(None, None, "tensor"),
        P(None, "tensor", None),
        P(),
    )
    return jax.shard_map(
        on_device,
        mesh=mesh,
        in_specs=placed,
        out_specs=(
            P(("dp", "tensor"), None),
            P(("dp", "tensor"), None),
            P(),
            P(None, None, None, "tensor"),
            P(None, "tensor", None),
            P(),
            P(),
            P(None, None, "tensor"),
            P(None, "tensor", None),
            P(),
        ),
        check_vma=False,
    )
```

time: 941 us -> 497 us (0.53); the launches traced: 930 us -> 496 us
  local copies, waits for them, and re-layouts: 291 us -> 32.2 us
  Pallas kernels: 0 us -> 199 us
  matrix products: 184 us -> 7.39 us
  blocking collectives: 140 us -> 0 us
  other arithmetic: 61.4 us -> 16.6 us
    pallas_call x0 -> x1, Pallas kernels: none -> 199 us  [call_kernel(): pl.pallas_call(kernel, out_shape=(sds((R, D), BF), sds((R, D), BF), sds((...]
    dot_general x44 -> x4, matrix products: 184 us -> 7.39 us  [the longest x2 7.15 us: on_device(): jnp.einsum('ai,i...->a...', slots, v, precision=lax.Precision.HIGHEST)]
    unnamed x3 -> x0, blocking collectives: 140 us -> none
    add x7 -> x0, local copies, waits for them, and re-layouts: 99.8 us -> none  [the longest x6 99.8 us: window_scores(): base_scores.reshape(win_count, head_count, WIN, WIN, WIN, WIN)]
    all_gather x4 -> x0, waiting for transfers between devices: 87.6 us -> none  [the longest x1 33.4 us: on_device(): dy2 = lax.all_gather(dy2_local, 'tensor', axis=0, tiled=True)]
    unnamed x160 -> x53, local copies, waits for them, and re-layouts: 66.6 us -> 9.82 us
    psum x2, waiting for transfers between devices: 139 us -> 193 us  [the longest x1 123 us: on_device(): whole = lax.psum(mine[:, None, None, None] * g_rep[None], ('dp', 'tensor'))]
    reshape x8 -> x10, local copies, waits for them, and re-layouts: 50.7 us -> 7.47 us  [the longest x1 1.74 us: on_device(): jnp.stack([out, grad]).reshape(2, NW, PAD, D)[:, :, :TOK]]
  transfers between devices with their start and end apart: 10 -> 5, of which waited for: 7 -> 3; matrix products, arithmetic and copies ran while one was open for 16% -> 7% of each run, Pallas kernels for 0% -> 0%
where the time goes in v1:
time: 497 us; the launch traced here: 496 us
  waiting for transfers between devices  221 us (44%)
  Pallas kernels  199 us (40%)
  local copies, waits for them, and re-layouts  32.2 us (6%)
  other arithmetic  16.6 us (3%)
  between operations  16.2 us (3%)
  matrix products  7.39 us (1%)
    pallas_call x1, Pallas kernels, call_kernel(): pl.pallas_call(kernel, out_shape=(sds((R, D), BF), sds((R, D), BF), sds((...  199 us
    psum x1, waiting for transfers between devices, on_device(): whole = lax.psum(mine[:, None, None, None] * g_rep[None], ('dp', 'tensor'))  123 us
    psum x1, waiting for transfers between devices, on_device(): split = lax.psum(mine[:, None] * split[None], 'dp')  69.8 us
    unnamed x4, waiting for transfers between devices  28.8 us
  transfers between devices with their start and end apart: 5, of which 3 were waited for; matrix products, arithmetic and copies ran while one was open for 7% of the time, Pallas kernels for 0%

profile of v1, /device:TPU:0, one launch (start us, length us, event | category | flops | bytes accessed | tf_op | source)
XLA Modules:
  0.0 496.4 jit_solution(2752914544711016243)
XLA Ops:
  7.4 1.3 pad_maximum_fusion.2
  8.7 0.6 copy.84
  9.3 1.3 collective-permute-start
  10.6 0.1 reshape.270
  10.7 0.6 fusion.44
  13.3 0.8 constant_dynamic-slice_fusion.2
  14.1 0.1 reshape.269
  14.2 0.7 dynamic-slice_bitcast_fusion.4
  14.9 0.8 dynamic-slice_bitcast_fusion.3
  15.8 0.1 stack.74
  15.9 0.6 pad_convert_fusion.vec_ref
  16.5 0.1 pad.48.clone
  16.6 0.1 pad.51.clone
  16.7 0.1 pad.54.clone
  16.8 0.1 pad_dynamic-slice_fusion.5
  16.9 1.3 and_select_fusion.valid_ref
  18.2 0.1 fusion.57
  18.4 0.6 dynamic-slice
  19.0 0.1 convolution_add_fusion
  19.2 0.8 concatenate.38.pack_hbm
  19.9 0.1 pad_bitcast_fusion
  20.1 0.8 pad_maximum_fusion.3.rel_ref
  20.9 0.8 constant_dynamic-slice_fusion
  21.7 0.8 dynamic-slice_bitcast_fusion
  22.5 0.7 fusion.10.adp_ref
  23.2 1.2 copy.85
  24.5 3.5 fusion.2
  27.9 1.7 reshape.267
  29.7 1.5 pad_slice_fusion
  31.2 198.7 %block.1 = (bf16[416,1280]{1,0:T(8,128)(2,1)}, bf16[416,1280]{1,0:T(8,128)(2,1)}, f32[4,16,1280]{2,1,0:T(8,128)}, f32[4,3,16,320]{3,2,1,0:T(8,128)}, f32[4,16,32...) custom-call(bf16[416,1280]{1,0:T(8,128)(2,1)} %bitcast.84, bf16[416,1280]{1,0:T(8,128)(2,1)} %bitcast.83, ...), custom_call_target="tpu_custom_call" | custom-call | tf_op jit(solution)/shard_map/block/pallas_call | solution.py:548
  229.9 3.0 pad_maximum_fusion
  232.9 1.7 reshape.272
  234.7 0.2 slice.32
  234.9 1.5 copy.90
  236.3 2.2 collective-permute-start.1
  238.5 1.1 broadcast_multiply_fusion
  239.7 0.0 all-reduce.16.cloned.1.call-start
  239.7 0.9 copy.102
  240.7 0.9 copy.101
  241.6 0.1 reshape.274
  241.7 0.9 reshape.273
  242.6 1.4 pad_maximum_fusion.1
  244.0 2.0 gather_fusion
  246.0 0.3 all-reduce.14.cloned.1.call-start
  246.3 122.8 %all-reduce.12.cloned.1.call-done = f32[2,4,16,1280]{3,0,2,1:T(2,128)} async-done(((f32[2,4,16,1280]{3,0,2,1:T(2,128)}), f32[2,4,16,1280]{3,0,2,1:T(2,128)}) %all-reduce.12.cloned.1.call-update) | async-done | bytes 655376 | tf_op jit(solution)/shard_map/psum | solution.py:689
  369.0 4.0 fusion.41
  373.1 0.2 slice_bitcast_fusion.2
  373.3 1.0 copy.93
  374.4 1.0 copy.94
  375.4 1.0 copy.95
  376.4 1.0 copy.97
  377.5 28.8 %all-reduce.16.cloned.1.call-done = f32[4,61440]{1,0:T(4,128)} async-done(((f32[4,61440]{1,0:T(4,128)}), f32[4,61440]{1,0:T(4,128)}) %all-reduce.16.cloned.1.call-update) | async-done | bytes 983056
  406.3 2.1 constant_dynamic-slice_fusion.3
  408.3 1.0 broadcast_multiply_fusion.1
  409.4 1.2 copy.91
  410.6 1.0 fusion.3
  411.6 1.3 slice_bitcast_fusion
  412.9 69.8 %all-reduce.14.cloned.1.call-done = f32[2,61440]{1,0:T(2,128)} async-done(((f32[2,61440]{1,0:T(2,128)}), f32[2,61440]{1,0:T(2,128)}) %all-reduce.14.cloned.1.call-update) | async-done | bytes 491536 | tf_op jit(solution)/shard_map/psum | solution.py:688
  482.7 3.1 fusion.43
  485.9 0.1 fusion.56
  486.0 1.0 reshape.277
  487.0 0.8 reshape.278
  487.8 1.0 copy.96
  488.8 1.0 copy.104
  (77 shorter events, 0.4 us)
Async XLA Ops:
  7.2 7.7 %copy-start = (bf16[8,1280,16]{1,2,0:T(8,128)(2,1)S(1)}, bf16[8,1280,16]{1,2,0:T(8,128)(2,1)}, u32[]{:S(2)}) copy-start(bf16[8,1280,16]{1,2,0:T(8,128)(2,1)} %param.54) | copy-start | bytes 983044
  7.2 361.8 %all-reduce.12.cloned.1.call-start = ((), (), s32[]{:S(2)}) async-start(), calls=%async_computation | async-start | bytes 1310720 | tf_op jit(solution)/shard_map/psum | solution.py:689
  7.2 3.4 copy-start.19
  7.3 3.4 copy-start.20
  7.3 7.6 %copy-start.12 = (bf16[1280]{0:T(1024)(128)(2,1)S(1)}, bf16[1280]{0:T(1024)(128)(2,1)}, u32[]{:S(2)}) copy-start(bf16[1280]{0:T(1024)(128)(2,1)} %param.45) | copy-start | bytes 7684
  7.3 8.4 %copy-start.13 = (bf16[1280]{0:T(1024)(128)(2,1)S(1)}, bf16[1280]{0:T(1024)(128)(2,1)}, u32[]{:S(2)}) copy-start(bf16[1280]{0:T(1024)(128)(2,1)} %param.34) | copy-start | bytes 7684
  7.3 8.4 %copy-start.14 = (bf16[1280]{0:T(1024)(128)(2,1)S(1)}, bf16[1280]{0:T(1024)(128)(2,1)}, u32[]{:S(2)}) copy-start(bf16[1280]{0:T(1024)(128)(2,1)} %param.35) | copy-start | bytes 7684
  7.3 8.5 %copy-start.15 = (bf16[1280]{0:T(1024)(128)(2,1)S(1)}, bf16[1280]{0:T(1024)(128)(2,1)}, u32[]{:S(2)}) copy-start(bf16[1280]{0:T(1024)(128)(2,1)} %param.42) | copy-start | bytes 7684
  7.3 8.5 %copy-start.16 = (bf16[1280]{0:T(1024)(128)(2,1)S(1)}, bf16[1280]{0:T(1024)(128)(2,1)}, u32[]{:S(2)}) copy-start(bf16[1280]{0:T(1024)(128)(2,1)} %param.43) | copy-start | bytes 7684
  7.3 8.5 %copy-start.17 = (bf16[1280]{0:T(1024)(128)(2,1)S(1)}, bf16[1280]{0:T(1024)(128)(2,1)}, u32[]{:S(2)}) copy-start(bf16[1280]{0:T(1024)(128)(2,1)} %param.41) | copy-start | bytes 7684
  7.3 8.5 %copy-start.18 = (bf16[1280]{0:T(1024)(128)(2,1)S(1)}, bf16[1280]{0:T(1024)(128)(2,1)}, u32[]{:S(2)}) copy-start(bf16[1280]{0:T(1024)(128)(2,1)} %param.47) | copy-start | bytes 7684
  7.3 10.9 %copy-start.9 = (bf16[128,27]{1,0:T(8,128)(2,1)S(1)}, bf16[128,27]{1,0:T(8,128)(2,1)}, u32[]{:S(2)}) copy-start(bf16[128,27]{1,0:T(8,128)(2,1)} %constant.152.clone) | copy-start | bytes 20740
  7.3 10.9 %copy-start.10 = (bf16[27,80]{1,0:T(8,128)(2,1)S(1)}, bf16[27,80]{1,0:T(8,128)(2,1)}, u32[]{:S(2)}) copy-start(bf16[27,80]{1,0:T(8,128)(2,1)} %param.38) | copy-start | bytes 12964
  7.4 11.0 %copy-start.21 = (u32[32]{0:T(128)S(1)}, u32[32]{0:T(128)}, u32[]{:S(2)}) copy-start(u32[32]{0:T(128)} %constant.176) | copy-start | bytes 388
  7.4 11.6 %copy-start.8 = (bf16[128,27]{1,0:T(8,128)(2,1)S(1)}, bf16[128,27]{1,0:T(8,128)(2,1)}, u32[]{:S(2)}) copy-start(bf16[128,27]{1,0:T(8,128)(2,1)} %constant.153.clone) | copy-start | bytes 20740
  7.4 11.6 %copy-start.11 = (bf16[27,80]{1,0:T(8,128)(2,1)S(1)}, bf16[27,80]{1,0:T(8,128)(2,1)}, u32[]{:S(2)}) copy-start(bf16[27,80]{1,0:T(8,128)(2,1)} %param.39) | copy-start | bytes 12964
  9.3 14.0 %collective-permute-start = (bf16[2,147,1280]{2,0,1:T(2,128)(2,1)S(1)}, bf16[2,147,1280]{2,0,1:T(2,128)(2,1)}, u32[]{:S(2)}, u32[]{:S(2)}) collective-permute-start(bf16[2,147,1280]{2,0,1:T(2,128)(2,1)S(1)} %copy.84), channel_id=1, source_target_pairs={{1,0},{2,1},{3,2},{5,4},{6,5},{7,6},{9,8},{10,9},{11,10},{13,12},{... | collective-permute-start | bytes 2257928 | tf_op jit(solution)/shard_map/ppermute | solution.py:639
  19.1 5.3 %copy-start.1 = (bf16[343,1280]{1,0:T(8,128)(2,1)S(1)}, bf16[343,1280]{1,0:T(8,128)(2,1)}, u32[]{:S(2)}) copy-start(bf16[343,1280]{1,0:T(8,128)(2,1)} %param.31) | copy-start | bytes 2634244
  19.1 5.3 %copy-start.2 = (bf16[343,1280]{1,0:T(8,128)(2,1)S(1)}, bf16[343,1280]{1,0:T(8,128)(2,1)}, u32[]{:S(2)}) copy-start(bf16[343,1280]{1,0:T(8,128)(2,1)} %param.32) | copy-start | bytes 2634244
  234.7 3.9 copy-start.3
  234.7 5.1 %copy-start.5 = (f32[4,16,1280]{2,1,0:T(8,128)S(1)}, f32[4,16,1280]{2,1,0:T(8,128)}, u32[]{:S(2)}) copy-start(f32[4,16,1280]{2,1,0:T(8,128)} %get-tuple-element.23) | copy-start | bytes 983044
  234.9 5.8 %copy-start.4 = (f32[4,16,1280]{2,1,0:T(8,128)S(1)}, f32[4,16,1280]{2,1,0:T(8,128)}, u32[]{:S(2)}) copy-start(f32[4,16,1280]{2,1,0:T(8,128)} %get-tuple-element.22) | copy-start | bytes 983044
  234.9 6.7 %copy-start.7 = (f32[4,16,320]{2,1,0:T(8,128)S(1)}, f32[4,16,320]{2,1,0:T(8,128)}, u32[]{:S(2)}) copy-start(f32[4,16,320]{2,1,0:T(8,128)} %get-tuple-element.21) | copy-start | bytes 245764
  234.9 6.8 %copy-start.6 = (f32[4,3,16,320]{3,2,1,0:T(8,128)S(1)}, f32[4,3,16,320]{3,2,1,0:T(8,128)}, u32[]{:S(2)}) copy-start(f32[4,3,16,320]{3,2,1,0:T(8,128)} %get-tuple-element.20) | copy-start | bytes 737284
  236.3 173.0 %collective-permute-start.1 = (bf16[2,147,1280]{2,0,1:T(2,128)(2,1)}, bf16[2,147,1280]{2,0,1:T(2,128)(2,1)}, u32[]{:S(2)}, u32[]{:S(2)}) collective-permute-start(bf16[2,147,1280]{2,0,1:T(2,128)(2,1)} %copy.90), channel_id=1, source_target_pairs={{0,1},{1,2},{2,3},{4,5},{5,6},{6,7},{8,9},{9,10},{10,11},{12,13},{... | collective-permute-start | bytes 2257928 | tf_op jit(solution)/shard_map/ppermute | solution.py:676
  239.7 166.6 %all-reduce.16.cloned.1.call-start = ((), (), s32[]{:S(2)}) async-start(), calls=%async_computation.2 | async-start | bytes 1966080
  246.0 236.8 %all-reduce.14.cloned.1.call-start = ((), (), s32[]{:S(2)}) async-start(), calls=%async_computation.1 | async-start | bytes 983040 | tf_op jit(solution)/shard_map/psum | solution.py:688
Sparse Core Ops, SparseCore 0:
  239.8 129.1 all-reduce.11
  371.6 34.6 all-reduce.15
  410.2 72.4 all-reduce.13

commit v2 on v1

--- a/solution.py
+++ b/solution.py
@@ -26,6 +26,7 @@
 HID = 1280
 HC = 256
 PACK = 3584
+ROWS = 352
 EXT = 32
 HALF = 0.5
 EPS = 1e-6
@@ -63,12 +64,18 @@
 
 
 class Wire:
-    def __init__(self, own, land, pack_own, pack_land, sems):
+    def __init__(self, own, land, pack_own, pack_land, sems, images):
         self.own, self.land, self.sems = own, land, sems
         self.pack_own, self.pack_land = pack_own, pack_land
         dp, t = lax.axis_index("dp"), lax.axis_index("tensor")
         self.q = lax.rem(dp, 4)
-        self.dev = {"x": (dp ^ 1, t), "z": (dp ^ 2, t), "y": (dp, t ^ 2), "c": (dp, t ^ 1)}
+        self.t = t
+        self.image = dp // GROUP
+        self.levels = images.bit_length() - 1
+        self.dev = {"x": (dp ^ 1, t), "z": (dp ^ 2, t), "d": (dp ^ 3, t)}
+        self.dev |= {"c": (dp, t ^ 1), "y": (dp, t ^ 2), "yc": (dp, t ^ 3)}
+        self.dev |= {f"i{b}": (dp ^ (GROUP << b), t) for b in range(self.levels)}
+        self.near = {"next": (dp, lax.rem(t + 1, 4)), "prev": (dp, lax.rem(t + 3, 4))}
         self.count = {}
 
     def barrier(self):
@@ -84,9 +91,26 @@
             dst_ref=dst,
             send_sem=self.sems.at[0, n],
             recv_sem=self.sems.at[1, n],
-            device_id=self.dev[dev],
+            device_id=(self.dev | self.near)[dev],
             device_id_type=MESH,
         )
+
+    def ready(self, sem):
+        for d in self.dev.values():
+            pl.semaphore_signal(sem, inc=1, device_id=d, device_id_type=MESH)
+
+    def all_ready(self, sem):
+        pl.semaphore_wait(sem, len(self.dev))
+
+    def edge(self, key, src, dst, forward, do):
+        for s in range(1, 4):
+            n = 16 * -(-49 * s // 16)
+            at, to = (s - 1, s) if forward else (s, s - 1)
+
+            @pl.when(self.t == (at if do != "wait" else to))
+            def _():
+                cp = self.copy((key, s), src(n), dst(n), "next" if forward else "prev")
+                getattr(cp, {"go": "start", "wait": "wait_recv", "end": "wait_send"}[do])()
 
     def pack(self, what):
         return {
@@ -174,6 +198,126 @@
                 self.piece(c, w).wait_send()
 
 
+class Sum:
+    def __init__(self, wire, name, send, buf, images):
+        self.wire, self.name, self.send, self.buf, self.images = wire, name, send, buf, images
+        self.n = send.shape[1]
+
+    def go(self, key, src, dst, dev, do):
+        cp = self.wire.copy((self.name, key), src, dst, dev)
+        getattr(cp, {"go": "start", "wait": "wait_recv", "end": "wait_send"}[do])()
+
+    def first(self, k, rows, do):
+        dev = {1: "c", 2: "y", 3: "yc"}[k]
+        dst = self.buf.at[1, pl.ds((k - 1) * self.n + rows.start, rows.size)]
+        self.go(("a", k, rows.start), self.send.at[k, rows], dst, dev, do)
+
+    def second(self, do):
+        n = self.n
+        for j, dev in enumerate("xzd"):
+            src, dst = self.buf.at[1, pl.ds(3 * n, n)], self.buf.at[1, pl.ds((4 + j) * n, n)]
+            self.go(("b", j), src, dst, dev, do)
+
+    def third(self, level, do):
+        n, size = self.n, 1 << level
+        start = (self.wire.image >> level) << level
+        if do == "wait":
+            start = start ^ size
+        rows = pl.ds(mult(start * n), size * n)
+        self.go(("i", level), self.buf.at[2, rows], self.buf.at[2, rows], f"i{level}", do)
+
+    def fourth(self, do):
+        m, t = self.images * RANK, self.wire.t
+        for k in (1, 2, 3):
+            owner = t if do != "wait" else t ^ k
+            part = self.buf.at[3, pl.ds(mult(owner * m), m), pl.ds(0, D // 2)]
+            self.go(("r", k), part, part, {1: "c", 2: "y", 3: "yc"}[k], do)
+
+    def finish(self, split):
+        for k in (1, 2, 3):
+            for rows in split:
+                self.first(k, rows, "end")
+        self.second("end")
+        for b in range(self.wire.levels):
+            self.third(b, "end")
+        self.fourth("end")
+
+    def part(self, slab, i):
+        return self.buf[slab, i * self.n : (i + 1) * self.n, :].astype(F32)
+
+    def add_first(self, split):
+        for k in (1, 2, 3):
+            for rows in split:
+                self.first(k, rows, "wait")
+        total = self.send[0].astype(F32) + self.part(1, 0) + self.part(1, 1) + self.part(1, 2)
+        self.buf[1, 3 * self.n : 4 * self.n, :] = total.astype(BF)
+        self.second("go")
+
+    def add_second(self):
+        self.second("wait")
+        total = self.part(1, 3) + self.part(1, 4) + self.part(1, 5) + self.part(1, 6)
+        self.buf[2, pl.ds(mult(self.wire.image * self.n), self.n), :] = total.astype(BF)
+        if self.wire.levels:
+            self.third(0, "go")
+
+    def add_third(self):
+        for b in range(self.wire.levels):
+            self.third(b, "wait")
+            if b + 1 < self.wire.levels:
+                self.third(b + 1, "go")
+        n, m = self.n, self.images * RANK
+        for i in range(self.images):
+            own = pl.ds(mult(self.wire.t * m + i * RANK), RANK)
+            self.buf[3, own, 0 : D // 2] = self.buf[
+                2, (i + 1) * n - RANK : (i + 1) * n, 0 : D // 2
+            ]
+        self.fourth("go")
+
+    def hand_out(self, split_out, whole_out, local):
+        self.fourth("wait")
+        n, m = self.n, self.images * RANK
+        copies = [
+            pltpu.make_async_copy(self.buf.at[2, 0 : self.images * n], split_out, local.at[0]),
+            pltpu.make_async_copy(self.buf.at[3, 0 : 4 * m, 0 : D // 2], whole_out, local.at[1]),
+        ]
+        for cp in copies:
+            cp.start()
+        return copies
+
+
+def half_of(ref, wire, k):
+    s = wire.t ^ k
+    return ref[s >> 1, :, pl.ds(mult((s & 1) * (D // 2), 128), D // 2)]
+
+
+def one_hot(target, count):
+    lane = lax.broadcasted_iota(jnp.int32, (target.shape[0], count), 1)
+    return jnp.where(lane == target, 1.0, 0.0).astype(BF)
+
+
+def window_rows(t):
+    r = lax.broadcasted_iota(jnp.int32, (R, 1), 0)
+    w = jnp.where(r >= PAD, 1, 0)
+    i = r - PAD * w
+    p = 49 * t + TOK * w + i
+    source = jnp.where(i < TOK, jnp.where(p < 343, p, p + (ROWS - 343)), -1)
+    slot = lax.rem(lax.axis_index("dp"), GROUP) * WIN_DEV + NW * t + w
+    high = (slot * 205) >> 10
+    row = (i * 4682) >> 16
+    ok = (i < TOK) & (NW * t + w < WIN_DEV) & (slot < GRID * GRID)
+    ok = ok & (high * WIN + row < SIDE) & ((slot - GRID * high) * WIN + i - WIN * row < SIDE)
+    return source, jnp.where(ok, 1.0, 0.0).astype(F32)
+
+
+def home_rows(t, mine, fetched):
+    r = lax.broadcasted_iota(jnp.int32, (ROWS, 1), 0)
+    o = r - 49 * t
+    here = jnp.where(o < 0, -1, jnp.where(o < TOK, o, o + PAD - TOK))
+    there = jnp.where(o < 0, r + 4 - t, -1)
+    here, there = one_hot(here, R), one_hot(there, 160)
+    return lambda cols: (nn(here, mine[:, cols]) + nn(there, fetched[:, cols])).astype(BF)
+
+
 STEPS = NCH + 2
 
 
@@ -233,23 +377,34 @@
 
 
 def kernel(
+    images,
     x_hbm, g_hbm, wq_hbm, wp_hbm, w1_hbm, w2_hbm, pack_hbm,
-    vec_ref, adp_ref, valid_ref, shift_ref, rel_ref, hot_ref, back_ref, key_ref,
-    out_hbm, grad_hbm, g_rep, g_bq, g_ap, g_b1, g_a2,
+    vec_ref, adp_ref, shift_ref, rel_ref, hot_ref, back_ref, key_ref,
+    out_hbm, grad_hbm, split_1, whole_1, split_2, whole_2,
     x_s, g_s, wq, wp, w1, w2, pack, xn_s, q_s, k_s, v_s, att_s, p_s, mid_s, acc_a, acc_b,
-    datt_s, d1t_s, up2t_s, d1_s, up2_s, d2_s, up1_s, upq_s, dqt_s, sems, local,
+    datt_s, d1t_s, up2t_s, d1_s, up2_s, d2_s, up1_s, upq_s, dqt_s, valid_ref, sum_1, sum_2,
+    rep_s, sems, local, done,
 ):
     own = {"q": wq_hbm, "p": wp_hbm, "1": w1_hbm, "2": w2_hbm}
     land = {"q": wq, "p": wp, "1": w1, "2": w2}
-    wire = Wire(own, land, pack_hbm, pack, sems)
+    wire = Wire(own, land, pack_hbm, pack, sems, images)
+    total_1 = Sum(wire, "s1", sum_1, w1, images)
+    total_2 = Sum(wire, "s2", sum_2, w2, images)
+    t = wire.t
+    blank = jnp.zeros((512 - ROWS, D), BF)
+    w1[0, ROWS:512, :] = blank
+    w2[0, ROWS:512, :] = blank
     wire.barrier()
-    wire.begin()
+    for key, src, dst in (("ex", x_hbm, w1), ("eg", g_hbm, w2)):
+        wire.edge(key, lambda n: src.at[0:n], lambda n: dst.at[0, ROWS : ROWS + n], False, "go")
+        if key == "ex":
+            wire.begin()
     pairs = [
-        (x_hbm, x_s), (pack_hbm, pack.at[0]), (wq_hbm, wq.at[0]), (wp_hbm, wp.at[0]),
-        (g_hbm, g_s), (w1_hbm, w1.at[0]), (w2_hbm, w2.at[0]),
+        (x_hbm, w1.at[0, 0:ROWS]), (pack_hbm, pack.at[0]), (wq_hbm, wq.at[0]),
+        (wp_hbm, wp.at[0]), (g_hbm, w2.at[0, 0:ROWS]), (w1_hbm, w1.at[0]), (w2_hbm, w2.at[0]),
     ]
     loads = [pltpu.make_async_copy(a, b, local.at[i]) for i, (a, b) in enumerate(pairs)]
-    for cp in loads:
+    for cp in loads[:5]:
         cp.start()
     lane_pad = jnp.zeros((4, R, LP - 256), BF)
     for ref in (q_s, k_s, v_s, att_s):
@@ -260,9 +415,16 @@
     bias_p, bias_2 = vec_ref[4:5, :], vec_ref[5:6, :]
     a_q, a_1, b_p, b_2 = (adp_ref[i] for i in range(4))
     lane_e = lax.broadcasted_iota(jnp.int32, (R, EXT), 1)
-    valid = valid_ref[...]
+    source, valid = window_rows(t)
+    valid_ref[...] = valid
+    pick_rows = one_hot(source, 512)
 
     loads[0].wait()
+    wire.edge("ex", lambda n: x_hbm.at[0:n], lambda n: w1.at[0, ROWS : ROWS + n], False, "wait")
+    for n in range(5):
+        cols = slice(256 * n, 256 * n + 256)
+        x_s[:, cols] = nn(pick_rows, w1[0, 0:512, cols]).astype(BF)
+    loads[5].start()
 
     def norm_one(rows):
         xhat, _ = stats(x_s[rows, :].astype(F32))
@@ -354,6 +516,13 @@
     d1_s[...] = jnp.where(lane_e == RANK, 1.0, down_1).astype(BF)
     d1t_s[...] = down_1.T.astype(BF)
     loads[4].wait()
+    wire.edge("eg", lambda n: g_hbm.at[0:n], lambda n: w2.at[0, ROWS : ROWS + n], False, "wait")
+    pick_rows = one_hot(window_rows(t)[0], 512)
+    for n in range(5):
+        cols = slice(256 * n, 256 * n + 256)
+        g_s[:, cols] = nn(pick_rows, w2[0, 0:512, cols]).astype(BF)
+    loads[6].start()
+    valid = valid_ref[...]
     up2 = HALF * valid * nt(g_s[...], b_2)
     up2_s[...] = up2.astype(BF)
     up2t_s[...] = up2.T.astype(BF)
@@ -399,11 +568,11 @@
         act = (pre * phi).astype(BF)
         slope = phi + pre * gauss * 0.3989422804014327
         a2 = pack[k, :, acols]
-        g_a2[k, :, cols] = nn(up2t_s[...], act)[:RANK]
+        sum_1[k, RANK : 2 * RANK, cols] = nn(up2t_s[...], act)[:RANK].astype(BF)
         d2_s[...] += nt(act, a2)
-        dact = valid * nt(g_s[...], w2[k, cols, :]) + nn(up2_s[...], a2)
+        dact = valid_ref[...] * nt(g_s[...], w2[k, cols, :]) + nn(up2_s[...], a2)
         dpre = (dact * slope).astype(BF)
-        g_b1[k, :, cols] = nn(d1t_s[...], dpre)[:RANK]
+        sum_1[k, 0:RANK, cols] = nn(d1t_s[...], dpre)[:RANK].astype(BF)
         up1_s[...] += nt(dpre, pack[k, :, pcols])
         for n in range(5):
             out = slice(256 * n, 256 * n + 256)
@@ -413,12 +582,23 @@
 
     lax.fori_loop(0, 20, hidden, 0)
 
+    wire.finish()
+    wire.edge("ex", lambda n: x_hbm.at[0:n], lambda n: w1.at[0, ROWS : ROWS + n], False, "end")
+    wire.edge("eg", lambda n: g_hbm.at[0:n], lambda n: w2.at[0, ROWS : ROWS + n], False, "end")
+    wire.ready(done)
     d2 = HALF * d2_s[...]
     d2b = d2.astype(BF)
     up1 = HALF * up1_s[...]
     up1b = up1.astype(BF)
-    g_rep[3] = nn((d2 * valid).T.astype(BF), g_s[...])[:RANK]
-    g_rep[2] = nn(up1.T.astype(BF), xn_s[...])[:RANK]
+    rep_s[1] = nn((d2 * valid_ref[...]).T.astype(BF), g_s[...])[:RANK].astype(BF)
+    rep_s[0] = nn(up1.T.astype(BF), xn_s[...])[:RANK].astype(BF)
+    for k in range(4):
+        sum_1[k, 2 * RANK :, 0 : D // 2] = half_of(rep_s, wire, k)
+        sum_1[k, 2 * RANK :, D // 2 :] = jnp.zeros((RANK, D // 2), BF)
+    wire.all_ready(done)
+    all_1 = pl.ds(0, 3 * RANK)
+    for k in (1, 2, 3):
+        total_1.first(k, all_1, "go")
     for n in range(5):
         cols = slice(256 * n, 256 * n + 256)
         acc_a[:, cols] += nn(d2b, b_2[:, cols])
@@ -435,21 +615,47 @@
         xn_s[rows, :] = x_out.astype(BF)
 
     row_loop(back_two)
-    put_out = pltpu.make_async_copy(xn_s, out_hbm, local.at[7])
-    put_out.start()
+
+    def swap_edge(key, src, dst, do):
+        to = lambda n: dst.at[0, 512 : 512 + n]
+        wire.edge(key, lambda n: src.at[R - n : R], to, True, do)
+
+    swap_edge("eo", xn_s, w1, "go")
     upp = HALF * nt(g_s[...], b_p)
     upp16 = upp[:, :RANK].astype(BF)
     uppt = upp.T.astype(BF)
-    g_rep[1] = nn(dpt, g_s[...])
+    rep_s[1] = nn(dpt, g_s[...]).astype(BF)
     acc_a[...] = jnp.zeros((R, D), F32)
     upq_s[...] = jnp.zeros((R, EXT), F32)
     up2_s[:, 0:RANK] = upp16
     up2t_s[...] = uppt
 
-    def heads_backward(k, _):
+    put_out = pltpu.make_async_copy(w1.at[0, 0:ROWS], out_hbm, local.at[7])
+
+    def heads_backward(step, _):
+        k = lax.rem(step + 1, 4)
+
+        @pl.when(step == 1)
+        def _():
+            total_1.add_first([all_1])
+            swap_edge("eo", xn_s, w1, "wait")
+            home = home_rows(t, xn_s, w1.at[0, 512:672])
+            for n in range(5):
+                cols = slice(256 * n, 256 * n + 256)
+                w1[0, 0:ROWS, cols] = home(cols)
+            put_out.start()
+
+        @pl.when(step == 2)
+        def _():
+            total_1.add_second()
+
+        @pl.when(step == 3)
+        def _():
+            total_1.add_third()
+
         datt = nt(g_s[...], wp[k]) + nn(up2_s[:, 0:RANK], pack[k, 16:32, 2304 : 2304 + LOC])
         datt_s[:, 0:LOC] = datt.astype(BF)
-        g_ap[k] = nn(up2t_s[...], att_s[k, :, 0:LOC])[:RANK]
+        sum_2[k, 0:RANK, 3 * LOC :] = nn(up2t_s[...], att_s[k, :, 0:LOC])[:RANK].astype(BF)
 
         def window(w, _):
             rows = pl.ds(mult(w * PAD), PAD)
@@ -478,17 +684,26 @@
             d = ref[k, :, 0:LOC]
             b = pack[k, :, j * LOC : (j + 1) * LOC]
             upq_s[...] += nt(d, b)
-            g_bq[k, j] = nn(dqt_s[...], d)[:RANK]
+            sum_2[k, 0:RANK, j * LOC : (j + 1) * LOC] = nn(dqt_s[...], d)[:RANK].astype(BF)
         for n in range(5):
             cols = slice(256 * n, 256 * n + 256)
             total = acc_a[:, cols]
             for j, ref in enumerate((q_s, k_s, v_s)):
                 total += nn(ref[k, :, 0:LOC], wq[k, j * LOC : (j + 1) * LOC, cols])
             acc_a[:, cols] = total
+
+        for kk in (1, 2, 3):
+
+            @pl.when(k == kk)
+            def _():
+                total_2.first(kk, pl.ds(0, RANK), "go")
+
         return 0
 
     lax.fori_loop(0, 4, heads_backward, 0)
+    puts = total_1.hand_out(split_1, whole_1, local.at[9:11])
     put_out.wait()
+    swap_edge("eo", xn_s, w1, "end")
 
     upq = HALF * upq_s[...]
     upqb = upq.astype(BF)
@@ -505,11 +720,31 @@
         g_s[rows, :] = (mid_s[rows, :] + back).astype(BF)
 
     row_loop(back_one)
-    put_grad = pltpu.make_async_copy(g_s, grad_hbm, local.at[8])
+    swap_edge("ef", g_s, w2, "go")
+    rep_s[0] = nn(upqt, xn_s[...])[:RANK].astype(BF)
+    for k in range(4):
+        sum_2[k, RANK:, 0 : D // 2] = half_of(rep_s, wire, k)
+        sum_2[k, RANK:, D // 2 :] = jnp.zeros((RANK, D // 2), BF)
+    low, high = pl.ds(0, RANK), pl.ds(RANK, RANK)
+    for k in (1, 2, 3):
+        total_2.first(k, high, "go")
+    total_2.add_first([low, high])
+    swap_edge("ef", g_s, w2, "wait")
+    home = home_rows(t, g_s, w2.at[0, 512:672])
+    for n in range(5):
+        cols = slice(256 * n, 256 * n + 256)
+        w2[0, 0:ROWS, cols] = home(cols)
+    put_grad = pltpu.make_async_copy(w2.at[0, 0:ROWS], grad_hbm, local.at[8])
     put_grad.start()
-    g_rep[0] = nn(upqt, xn_s[...])[:RANK]
+    total_2.add_second()
+    total_2.add_third()
+    puts += total_2.hand_out(split_2, whole_2, local.at[11:13])
+    for cp in puts:
+        cp.wait()
     put_grad.wait()
-    wire.finish()
+    swap_edge("ef", g_s, w2, "end")
+    total_1.finish([all_1])
+    total_2.finish([low, high])
 
 
 def tables(rel_pos_h, rel_pos_w):
@@ -540,24 +775,23 @@
     return rel, jnp.asarray(hot, BF), jnp.asarray(back.T, BF), jnp.asarray(shift), jnp.asarray(key)
 
 
-def call_kernel(args):
+def call_kernel(images, args):
     any_ = pl.BlockSpec(memory_space=pl.ANY)
     vmem = pl.BlockSpec(memory_space=pltpu.VMEM)
     sds = jax.ShapeDtypeStruct
     V = pltpu.VMEM
     return pl.pallas_call(
-        kernel,
+        functools.partial(kernel, images),
         out_shape=(
-            sds((R, D), BF),
-            sds((R, D), BF),
-            sds((4, RANK, D), F32),
-            sds((4, 3, RANK, LOC), F32),
-            sds((4, RANK, LOC), F32),
-            sds((4, RANK, HID), F32),
-            sds((4, RANK, HID), F32),
+            sds((ROWS, D), BF),
+            sds((ROWS, D), BF),
+            sds((images * 3 * RANK, D), BF),
+            sds((4 * images * RANK, D // 2), BF),
+            sds((images * 2 * RANK, D), BF),
+            sds((4 * images * RANK, D // 2), BF),
         ),
-        in_specs=[any_] * 7 + [vmem] * 8,
-        out_specs=(any_, any_) + (vmem,) * 5,
+        in_specs=[any_] * 7 + [vmem] * 7,
+        out_specs=(any_,) * 6,
         scratch_shapes=[
             V((R, D), BF),
             V((R, D), BF),
@@ -584,8 +818,13 @@
             V((R, EXT), F32),
             V((R, EXT), F32),
             V((EXT, R), BF),
-            pltpu.SemaphoreType.DMA((2, 12 * NCH + 3)),
-            pltpu.SemaphoreType.DMA((9,)),
+            V((R, 1), F32),
+            V((4, 3 * RANK, D), BF),
+            V((4, 2 * RANK, D), BF),
+            V((2, RANK, D), BF),
+            pltpu.SemaphoreType.DMA((2, 12 * NCH + 60)),
+            pltpu.SemaphoreType.DMA((13,)),
+            pltpu.SemaphoreType.REGULAR,
         ],
         compiler_params=pltpu.CompilerParams(
             collective_id=0, has_side_effects=True, vmem_limit_bytes=66_500_000
@@ -621,10 +860,8 @@
     lin2_down,
     lin2_up,
 ):
-    tensor_size = lax.axis_size("tensor")
     images = adapter_index.shape[0]
     row_count = tokens.shape[0]
-    t = lax.axis_index("tensor")
     dp_place = lax.axis_index("dp")
     image = dp_place // GROUP
     pick = jnp.sum(jnp.where(jnp.arange(images) == image, adapter_index, 0))
@@ -632,26 +869,7 @@
     def select(table_all):
         return lax.dynamic_index_in_dim(table_all, pick, 0, keepdims=False)
 
-    work = NW * TOK
-    gap = work - row_count
-    far = gap * (tensor_size - 1)
-    both = jnp.stack([tokens, grad_out])
-    more = lax.ppermute(both[:, :far], "tensor", [(s, s - 1) for s in range(1, tensor_size)])
-    none = jnp.zeros((2, gap, D), BF)
-    both = lax.dynamic_slice_in_dim(jnp.concatenate([both, more, none], axis=1), gap * t, work, 1)
-    both = jnp.pad(both.reshape(2, NW, TOK, D), ((0, 0), (0, 0), (0, PAD - TOK), (0, 0)))
-    x, g = both.reshape(2, R, D)
-
-    place = jnp.arange(R, dtype=jnp.int32)
-    window = place // PAD + NW * t
-    slot = dp_place % GROUP * WIN_DEV + window
-    within = place % PAD
-    image_row = slot // GRID * WIN + within // WIN
-    image_col = slot % GRID * WIN + within % WIN
-    valid = (within < TOK) & (window < WIN_DEV) & (slot < GRID * GRID)
-    valid = valid & (image_row < SIDE) & (image_col < SIDE)
-    valid = jnp.where(valid, 1.0, 0.0).astype(F32)[:, None]
-
+    both = [jnp.pad(v, ((0, ROWS - v.shape[0]), (0, 0))) for v in (tokens, grad_out)]
     wq = jnp.transpose(qkv_weight, (1, 2, 0)).reshape(3 * LOC, D)
     row = lambda v: v.reshape(1, -1)
     bq = jnp.transpose(select(qkv_up), (0, 1, 2)).reshape(RANK, 3 * LOC)
@@ -667,45 +885,42 @@
     adps = jnp.stack([select(qkv_down).T, select(lin1_down).T, select(proj_up), select(lin2_up)])
     adps = jnp.pad(adps, ((0, 0), (0, EXT - RANK), (0, 0)))
     rel, hot, back, shift, key = tables(rel_pos_h, rel_pos_w)
-    out, grad, g_rep, g_bq, g_ap, g_b1, g_a2 = call_kernel(
-        (x, g, wq, proj_weight, lin1_weight, lin2_weight, pack,
-         vecs, adps, valid, shift, rel, hot, back, key)
+    out, grad, split_1, whole_1, split_2, whole_2 = call_kernel(
+        images,
+        (*both, wq, proj_weight, lin1_weight, lin2_weight, pack,
+         vecs, adps, shift, rel, hot, back, key),
     )
 
-    ends = jnp.stack([out, grad]).reshape(2, NW, PAD, D)[:, :, :TOK].reshape(2, work, D)
-    more = lax.ppermute(
-        ends[:, work - far :], "tensor", [(s, s + 1) for s in range(tensor_size - 1)]
+    split_1 = split_1.reshape(images, 3 * RANK, D)
+    split_2 = split_2.reshape(images, 2 * RANK, D)
+    whole_1, whole_2 = (
+        v.reshape(2, 2, images, RANK, D // 2).transpose(0, 2, 3, 1, 4).reshape(2, images, RANK, D)
+        for v in (whole_1, whole_2)
     )
-    ends = jnp.concatenate([more, ends], axis=1)
-    output, grad_tokens = lax.dynamic_slice_in_dim(ends, far - gap * t, row_count, 1)
-
-    order = t ^ jnp.arange(tensor_size)
-    split = jnp.concatenate(
-        [v.reshape(tensor_size, -1) for v in (g_bq, g_ap, g_b1, g_a2)], axis=1
-    )
-    split = lax.psum_scatter(split[order], "tensor", scatter_dimension=0, tiled=False)
-    mine = jnp.where(jnp.arange(images) == image, 1.0, 0.0).astype(F32)
-    split = lax.psum(mine[:, None] * split[None], "dp")
-    whole = lax.psum(mine[:, None, None, None] * g_rep[None], ("dp", "tensor"))
-    slots = jnp.where(
-        jnp.arange(ADAPTERS)[:, None] == adapter_index[None], 1.0, 0.0
-    ).astype(F32)
-    to_slots = lambda v: jnp.einsum("ai,i...->a...", slots, v, precision=lax.Precision.HIGHEST)
-    split, whole = to_slots(split), to_slots(whole)
-    sizes = np.cumsum([3 * RANK * LOC, RANK * LOC, RANK * HID])
-    s_bq, s_ap, s_b1, s_a2 = jnp.split(split, sizes, axis=1)
+
+    slots = jnp.arange(ADAPTERS)[:, None] == adapter_index[None]
+
+    def to_slots(v):
+        v = v.astype(F32)
+        total = 0.0
+        for i in range(images):
+            hit = slots[:, i].reshape((-1,) + (1,) * (v.ndim - 1))
+            total = total + jnp.where(hit, v[i][None], 0.0)
+        return total
+
     swap = lambda v: jnp.swapaxes(v, 1, 2)
+    up_q = split_2[:, :RANK, : 3 * LOC].reshape(images, RANK, 3, LOC)
     return (
-        output,
-        grad_tokens,
-        swap(whole[:, 0]),
-        jnp.swapaxes(s_bq.reshape(ADAPTERS, 3, RANK, LOC), 1, 2),
-        swap(s_ap.reshape(ADAPTERS, RANK, LOC)),
-        whole[:, 1],
-        swap(whole[:, 2]),
-        s_b1.reshape(ADAPTERS, RANK, HID),
-        swap(s_a2.reshape(ADAPTERS, RANK, HID)),
-        whole[:, 3],
+        out[:row_count],
+        grad[:row_count],
+        swap(to_slots(whole_2[0])),
+        to_slots(up_q),
+        swap(to_slots(split_2[:, :RANK, 3 * LOC :])),
+        to_slots(whole_2[1]),
+        swap(to_slots(whole_1[0])),
+        to_slots(split_1[:, :RANK]),
+        swap(to_slots(split_1[:, RANK : 2 * RANK])),
+        to_slots(whole_1[1]),
     )
 
 

time: 497 us -> 264 us (0.53)
  waiting for transfers between devices: 221 us -> 0 us
  Pallas kernels: 199 us -> 230 us
  local copies, waits for them, and re-layouts: 32.2 us -> 16.6 us
  between operations: 16.2 us -> 2.93 us
  matrix products: 7.39 us -> 1.77 us
  other arithmetic: 16.6 us -> 11 us
    psum x2 -> x0, waiting for transfers between devices: 193 us -> none  [the longest x1 123 us: on_device(): whole = lax.psum(mine[:, None, None, None] * g_rep[None], ('dp', 'tensor'))]
    pallas_call x1, Pallas kernels: 199 us -> 230 us  [call_kernel(): pl.pallas_call(functools.partial(kernel, images), out_shape=(sds((ROWS, D...]
    unnamed x4 -> x0, waiting for transfers between devices: 28.8 us -> none
    unnamed x53 -> x22, local copies, waits for them, and re-layouts: 9.82 us -> 0.09 us
    dot_general x2 -> x0, matrix products: 7.15 us -> none  [on_device(): jnp.einsum('ai,i...->a...', slots, v, precision=lax.Precision.HIGHEST)]
    reshape x7 -> x2, local copies, waits for them, and re-layouts: 7.28 us -> 0.26 us  [on_device(): v.reshape(2, 2, images, RANK, D // 2).transpose(0, 2, 3, 1, 4)]
    concatenate x3 -> x0, other arithmetic: 5.88 us -> none  [the longest x1 3.48 us: on_device(): jnp.concatenate([both, more, none], axis=1)]
  transfers between devices with their start and end apart: 5 -> 0, of which waited for: 3 -> 0; matrix products, arithmetic and copies ran while one was open for 7% -> 0% of each run, Pallas kernels for 0% -> 0%
where the time goes in v2:
time: 264 us; the launch traced here: 263 us
  Pallas kernels  230 us (87%)
  local copies, waits for them, and re-layouts  16.6 us (6%)
  other arithmetic  11 us (4%)
  between operations  2.93 us (1%)
    pallas_call x1, Pallas kernels, call_kernel(): pl.pallas_call(functools.partial(kernel, images), out_shape=(sds((ROWS, D...  230 us

profile of v2, /device:TPU:0, one launch (start us, length us, event | category | flops | bytes accessed | tf_op | source)
XLA Modules:
  0.0 262.6 jit_solution(1322163014297631227)
XLA Ops:
  0.6 0.0 copy-start
  0.7 0.0 copy-start.2
  0.7 0.0 copy-start.1
  0.7 1.4 fusion.15
  4.1 0.7 iota_compare_fusion.4
  4.8 0.1 pad.44.clone
  4.9 0.1 pad.47.clone
  5.0 0.1 pad.50.clone
  5.1 0.8 reshape.88
  5.9 0.7 stack.47
  6.6 0.7 stack.48
  7.2 0.7 stack.51
  7.9 0.7 stack.49
  8.6 0.7 stack.50
  9.3 0.7 reshape.89
  10.0 0.7 stack.52
  10.7 0.1 stack.53
  10.8 0.7 dynamic-slice_bitcast_fusion.4
  11.5 0.6 pad_convert_fusion.vec_ref
  12.1 0.9 fusion.21
  13.0 0.9 convolution_add_fusion
  13.9 0.8 constant_dynamic-slice_fusion.2
  14.7 0.1 reshape.87
  14.8 0.0 copy-done
  14.8 0.8 dynamic-slice_bitcast_fusion.2
  15.6 0.8 concatenate.27.pack_hbm
  16.4 0.8 dynamic-slice_bitcast_fusion
  17.2 0.8 constant_dynamic-slice_fusion
  18.0 0.7 fusion.6.adp_ref
  18.8 0.1 pad_bitcast_fusion
  18.9 0.8 pad_maximum_fusion.rel_ref
  19.7 0.0 copy-done.1
  19.7 1.0 pad.30.x_hbm
  20.7 0.0 copy-done.2
  20.7 1.0 pad.31.g_hbm
  21.7 230.3 %block.1 = (bf16[352,1280]{1,0:T(8,128)(2,1)}, bf16[352,1280]{1,0:T(8,128)(2,1)}, bf16[96,1280]{1,0:T(8,128)(2,1)}, bf16[128,640]{1,0:T(8,128)(2,1)}, bf16[64,12...) custom-call(bf16[352,1280]{1,0:T(8,128)(2,1)} %pad.30.x_hbm, bf16[352,1280]{1,0:T(8,128)(2,1)} %pad.31.g_hbm, ...), custom_call_target="tpu_custom_call" | custom-call | tf_op jit(solution)/shard_map/block/pallas_call | solution.py:783
  252.0 0.0 copy-start.5
  252.0 0.0 copy-start.4
  252.0 2.2 slice.112
  254.2 0.0 copy-start.6
  254.2 0.9 slice_convert_fusion.7
  255.1 0.9 slice_convert_fusion.6
  256.0 0.1 broadcast_in_dim.289
  256.1 0.1 broadcast_in_dim.293
  256.2 0.0 copy-start.3
  256.2 0.8 select_add_fusion.7
  257.0 0.0 copy-done.5
  257.0 0.1 copy.66
  257.1 0.0 copy-done.4
  257.1 0.1 copy.65
  257.3 0.1 slice_convert_fusion
  257.5 0.1 slice_convert_fusion.4
  257.8 0.0 copy-done.6
  257.8 0.9 select_add_fusion.6
  258.8 0.0 copy-done.3
  258.8 1.0 slice.113
  259.8 1.4 select_add_fusion
  261.2 1.4 select_add_fusion.1
  (34 shorter events, 0.3 us)
Async XLA Ops:
  0.6 14.2 %copy-start = (bf16[8,16,1280]{2,1,0:T(8,128)(2,1)S(1)}, bf16[8,16,1280]{2,1,0:T(8,128)(2,1)}, u32[]{:S(2)}) copy-start(bf16[8,16,1280]{2,1,0:T(8,128)(2,1)} %param.53) | copy-start | bytes 983044
  0.7 20.1 %copy-start.2 = (bf16[343,1280]{1,0:T(8,128)(2,1)S(1)}, bf16[343,1280]{1,0:T(8,128)(2,1)}, u32[]{:S(2)}) copy-start(bf16[343,1280]{1,0:T(8,128)(2,1)} %param.32) | copy-start | bytes 2634244
  0.7 19.1 %copy-start.1 = (bf16[343,1280]{1,0:T(8,128)(2,1)S(1)}, bf16[343,1280]{1,0:T(8,128)(2,1)}, u32[]{:S(2)}) copy-start(bf16[343,1280]{1,0:T(8,128)(2,1)} %param.31) | copy-start | bytes 2634244
  252.0 5.0 %copy-start.5 = (bf16[128,640]{1,0:T(8,128)(2,1)S(1)}, bf16[128,640]{1,0:T(8,128)(2,1)}, u32[]{:S(2)}) copy-start(bf16[128,640]{1,0:T(8,128)(2,1)} %get-tuple-element.18) | copy-start | bytes 491524
  252.0 5.1 %copy-start.4 = (bf16[128,640]{1,0:T(8,128)(2,1)S(1)}, bf16[128,640]{1,0:T(8,128)(2,1)}, u32[]{:S(2)}) copy-start(bf16[128,640]{1,0:T(8,128)(2,1)} %get-tuple-element.20) | copy-start | bytes 491524
  254.2 3.5 %copy-start.6 = (bf16[96,1280]{1,0:T(8,128)(2,1)S(1)}, bf16[96,1280]{1,0:T(8,128)(2,1)}, u32[]{:S(2)}) copy-start(bf16[96,1280]{1,0:T(8,128)(2,1)} %get-tuple-element.21) | copy-start | bytes 737284
  256.2 2.6 copy-start.3

commit v3 on v2

--- a/solution.py
+++ b/solution.py
@@ -25,7 +25,8 @@
 LP = 384
 HID = 1280
 HC = 256
-PACK = 3584
+PACK_Q = (3 * 32, 320)
+PACK_M = (32, 2560)
 ROWS = 352
 EXT = 32
 HALF = 0.5
@@ -39,12 +40,18 @@
 ERF_A = (0.254829592, -0.284496736, 1.421413741, -1.453152027, 1.061405429)
 
 CHUNKS = (
-    [("q", 0, 320), ("q", 320, 320), ("q", 640, 320), ("p", 0, 320)]
+    [("q", 192 * i, 192) for i in range(5)]
+    + [("p", 0, 320)]
     + [("1", 320 * i, 320) for i in range(4)]
     + [("2", 256 * i, 256) for i in range(5)]
 )
 NCH = len(CHUNKS)
-THIRDS = {80: ((2, 2, 1), (2, 1, 2), (1, 2, 2)), 64: ((2, 1, 1), (1, 2, 1), (1, 1, 2))}
+OF_Q, OF_P, OF_1, OF_2 = range(5), [5], range(6, 10), range(10, 15)
+THIRDS = {
+    80: ((2, 2, 1), (2, 1, 2), (1, 2, 2)),
+    64: ((2, 1, 1), (1, 2, 1), (1, 1, 2)),
+    48: ((1, 1, 1),) * 3,
+}
 
 
 def nn(a, b):
@@ -64,9 +71,9 @@
 
 
 class Wire:
-    def __init__(self, own, land, pack_own, pack_land, sems, images):
+    def __init__(self, own, land, packs, sems, images):
         self.own, self.land, self.sems = own, land, sems
-        self.pack_own, self.pack_land = pack_own, pack_land
+        self.packs = packs
         dp, t = lax.axis_index("dp"), lax.axis_index("tensor")
         self.q = lax.rem(dp, 4)
         self.t = t
@@ -112,12 +119,14 @@
                 cp = self.copy((key, s), src(n), dst(n), "next" if forward else "prev")
                 getattr(cp, {"go": "start", "wait": "wait_recv", "end": "wait_send"}[do])()
 
-    def pack(self, what):
-        return {
-            "c": lambda: self.copy("pc", self.pack_own, self.pack_land.at[1], "c"),
-            "y": lambda: self.copy("py", self.pack_own, self.pack_land.at[2], "y"),
-            "f": lambda: self.copy("pf", self.pack_land.at[2], self.pack_land.at[3], "c"),
-        }[what]()
+    def pack(self, what, do):
+        for i, (own, land) in enumerate(self.packs):
+            cp = {
+                "c": lambda: self.copy(("pc", i), own, land.at[1], "c"),
+                "y": lambda: self.copy(("py", i), own, land.at[2], "y"),
+                "f": lambda: self.copy(("pf", i), land.at[2], land.at[3], "c"),
+            }[what]()
+            getattr(cp, {"go": "start", "wait": "wait_recv", "end": "wait_send"}[do])()
 
     def parts(self, c):
         name, first, rows = CHUNKS[c]
@@ -129,11 +138,11 @@
             return pl.ds(mult(first + quart * quarter + off), n)
 
         return {
+            "all": pl.ds(first, rows),
             "y1": at(q, 0, quarter),
             "y2": at(q ^ 3, 0, a),
             "x1": at(q ^ 1, 0, quarter),
             "z1": at(q ^ 2, 0, quarter),
-            "d": at(q ^ 3, a, b + d),
             "xs": at(q, 0, quarter),
             "x2": at(q ^ 2, a, b),
             "z2": at(q ^ 1, a + b, d),
@@ -152,49 +161,47 @@
             return self.copy((c, what), land.at[2, p["xs"]], land.at[2, p["xs"]], what[0])
         if what in ("x2", "z2"):
             return self.copy((c, what), land.at[2, p[what]], land.at[2, p[what]], what[0])
-        r = p[what[1:]]
+        r = p["all"]
         return self.copy((c, what), land.at[2, r], land.at[3, r], "c")
 
-    def begin(self):
-        self.pack("c").start()
-        self.pack("y").start()
+    def begin(self, after_heads):
+        self.pack("c", "go")
         for c in range(NCH):
+            if c == OF_P[0]:
+                self.pack("y", "go")
+                after_heads()
             self.piece(c, "y1").start()
             self.piece(c, "y2").start()
             self.piece(c, "s").start()
 
-    def step(self, n):
-        if n == 0:
-            self.pack("y").wait_recv()
-            self.pack("f").start()
-        if n < NCH:
-            for w in ("y1", "y2"):
-                self.piece(n, w).wait_recv()
-            for w in ("x1", "z1", "cy1", "cy2"):
-                self.piece(n, w).start()
-        if 0 <= n - 1 < NCH:
-            for w in ("x1", "z1"):
-                self.piece(n - 1, w).wait_recv()
-            for w in ("x2", "z2", "cx1", "cz1"):
-                self.piece(n - 1, w).start()
-        if 0 <= n - 2 < NCH:
-            for w in ("x2", "z2"):
-                self.piece(n - 2, w).wait_recv()
-            self.piece(n - 2, "cd").start()
+    def step(self, what):
+        kind, n = what[0], int(what[1:])
+        if kind == "P":
+            self.pack("y", "wait")
+            self.pack("f", "go")
+            return
+        come, go = {
+            "A": (("y1", "y2"), ("x1", "z1")),
+            "B": (("x1", "z1"), ("x2", "z2")),
+            "C": (("x2", "z2"), ("f",)),
+        }[kind]
+        for w in come:
+            self.piece(n, w).wait_recv()
+        for w in go:
+            self.piece(n, w).start()
 
     def have(self, k, chunks):
         for c in chunks:
             if k == 1:
                 self.piece(c, "s").wait_recv()
             if k == 3:
-                for w in ("cy1", "cy2", "cx1", "cz1", "cd"):
-                    self.piece(c, w).wait_recv()
+                self.piece(c, "f").wait_recv()
 
     def finish(self):
         for w in "cyf":
-            self.pack(w).wait_send()
+            self.pack(w, "end")
         for c in range(NCH):
-            for w in ("s", "y1", "y2", "x1", "z1", "x2", "z2", "cy1", "cy2", "cx1", "cz1", "cd"):
+            for w in ("s", "y1", "y2", "x1", "z1", "x2", "z2", "f"):
                 self.piece(c, w).wait_send()
 
 
@@ -278,8 +285,12 @@
         n, m = self.n, self.images * RANK
         copies = [
             pltpu.make_async_copy(self.buf.at[2, 0 : self.images * n], split_out, local.at[0]),
-            pltpu.make_async_copy(self.buf.at[3, 0 : 4 * m, 0 : D // 2], whole_out, local.at[1]),
         ]
+        for s in range(4):
+            row, col = s // 2 * m, s % 2 * (D // 2)
+            src = self.buf.at[3, s * m : (s + 1) * m, 0 : D // 2]
+            dst = whole_out.at[row : row + m, col : col + D // 2]
+            copies.append(pltpu.make_async_copy(src, dst, local.at[1 + s]))
         for cp in copies:
             cp.start()
         return copies
@@ -318,9 +329,6 @@
     return lambda cols: (nn(here, mine[:, cols]) + nn(there, fetched[:, cols])).astype(BF)
 
 
-STEPS = NCH + 2
-
-
 def shifted(values, shift, right):
     for bit in (1, 2, 4, 8):
         moved = pltpu.roll(values, bit if right else 128 - bit, 1)
@@ -360,34 +368,46 @@
     )
 
 
-def row_loop(body, rows=32):
+def row_loop(body, rows=PAD):
     def one(i, _):
-        body(pl.ds(mult(i * rows, 32), rows))
+        body(pl.ds(mult(i * rows), rows))
         return 0
 
     lax.fori_loop(0, R // rows, one, 0)
 
 
 def ticks(wire, place, index):
-    for n, at in place.items():
+    for at, steps in place.items():
 
         @pl.when(index == at)
         def _():
-            wire.step(n)
+            for what in steps:
+                wire.step(what)
+
+
+AT_WINDOW = {
+    1: ("A0",), 2: ("A1", "B0"), 3: ("A2", "B1", "C0"), 5: ("A5",), 6: ("B5", "A6"), 7: ("C5",),
+}
+AT_SHARD = {2: ("A3", "B2", "C1", "A4", "B3", "C2", "B4", "C3", "C4")}
+AT_HIDDEN = {
+    0: ("A7", "B6", "A8"), 1: ("C6", "B7"), 3: ("A9", "B8", "C7"), 5: ("A10", "B9", "C8"),
+    7: ("A11", "B10", "C9"), 10: ("A12", "B11", "C10"), 12: ("A13", "B12", "C11"),
+    14: ("B13", "C12", "A14"), 16: ("B14", "C13"), 17: ("C14",),
+}
 
 
 def kernel(
     images,
-    x_hbm, g_hbm, wq_hbm, wp_hbm, w1_hbm, w2_hbm, pack_hbm,
-    vec_ref, adp_ref, shift_ref, rel_ref, hot_ref, back_ref, key_ref,
+    x_hbm, g_hbm, wq_hbm, wp_hbm, w1_hbm, w2_hbm, pq_hbm, pm_hbm,
+    vec_ref, adp_ref, shift_ref, row_ref, col_ref, hot_ref, back_ref, key_ref,
     out_hbm, grad_hbm, split_1, whole_1, split_2, whole_2,
-    x_s, g_s, wq, wp, w1, w2, pack, xn_s, q_s, k_s, v_s, att_s, p_s, mid_s, acc_a, acc_b,
-    datt_s, d1t_s, up2t_s, d1_s, up2_s, d2_s, up1_s, upq_s, dqt_s, valid_ref, sum_1, sum_2,
+    x_s, g_s, wq, wp, w1, w2, pack_q, pack_m, rel_ref, xn_s, q_s, k_s, v_s, att_s, p_s, mid_s, acc_a, acc_b,
+    datt_s, act_s, dpre_s, d1t_s, up2t_s, d1_s, up2_s, d2_s, up1_s, dqt_s, valid_ref, sum_1, sum_2,
     rep_s, sems, local, done,
 ):
     own = {"q": wq_hbm, "p": wp_hbm, "1": w1_hbm, "2": w2_hbm}
     land = {"q": wq, "p": wp, "1": w1, "2": w2}
-    wire = Wire(own, land, pack_hbm, pack, sems, images)
+    wire = Wire(own, land, [(pq_hbm, pack_q), (pm_hbm, pack_m)], sems, images)
     total_1 = Sum(wire, "s1", sum_1, w1, images)
     total_2 = Sum(wire, "s2", sum_2, w2, images)
     t = wire.t
@@ -395,26 +415,43 @@
     w1[0, ROWS:512, :] = blank
     w2[0, ROWS:512, :] = blank
     wire.barrier()
-    for key, src, dst in (("ex", x_hbm, w1), ("eg", g_hbm, w2)):
-        wire.edge(key, lambda n: src.at[0:n], lambda n: dst.at[0, ROWS : ROWS + n], False, "go")
-        if key == "ex":
-            wire.begin()
+
+    def edge_in(key, src, dst):
+        to = lambda n: dst.at[0, ROWS : ROWS + n]
+        wire.edge(key, lambda n: src.at[0:n], to, False, "go")
+
+    edge_in("ex", x_hbm, w1)
+    wire.begin(lambda: edge_in("eg", g_hbm, w2))
     pairs = [
-        (x_hbm, w1.at[0, 0:ROWS]), (pack_hbm, pack.at[0]), (wq_hbm, wq.at[0]),
+        (x_hbm, w1.at[0, 0:ROWS]), (pq_hbm, pack_q.at[0]), (wq_hbm, wq.at[0]),
         (wp_hbm, wp.at[0]), (g_hbm, w2.at[0, 0:ROWS]), (w1_hbm, w1.at[0]), (w2_hbm, w2.at[0]),
+        (pm_hbm, pack_m.at[0]),
     ]
     loads = [pltpu.make_async_copy(a, b, local.at[i]) for i, (a, b) in enumerate(pairs)]
-    for cp in loads[:5]:
+    for cp in loads[:5] + loads[7:]:
         cp.start()
     lane_pad = jnp.zeros((4, R, LP - 256), BF)
     for ref in (q_s, k_s, v_s, att_s):
         ref[:, :, 256:LP] = lane_pad
     datt_s[:, 256:LP] = lane_pad[0]
 
-    gain1, shift1, gain2, shift2 = (vec_ref[i : i + 1, :] for i in range(4))
-    bias_p, bias_2 = vec_ref[4:5, :], vec_ref[5:6, :]
-    a_q, a_1, b_p, b_2 = (adp_ref[i] for i in range(4))
+    vecs = vec_ref[...].astype(F32)
+    gain1, shift1, gain2, shift2, bias_p, bias_2 = (vecs[i : i + 1, :] for i in range(6))
+
+    def factor(i):
+        return jnp.concatenate([adp_ref[i], jnp.zeros((EXT - RANK, D), BF)], axis=0)
+
     lane_e = lax.broadcasted_iota(jnp.int32, (R, EXT), 1)
+    line = lax.broadcasted_iota(jnp.int32, (128, 2 * WIN - 1), 0)
+    lane = lax.broadcasted_iota(jnp.int32, (128, 2 * WIN - 1), 1)
+    rel = nn(jnp.where(line + lane == 2 * WIN - 2, 1.0, 0.0).astype(BF), row_ref[...])
+    rel += nn(jnp.where(line + lane == 64 + 2 * WIN - 2, 1.0, 0.0).astype(BF), col_ref[...])
+    rel = rel.astype(BF)
+    line = lax.broadcasted_iota(jnp.int32, (HEAD_DIM, LP), 0)
+    lane = lax.broadcasted_iota(jnp.int32, (HEAD_DIM, LP), 1)
+    for h in range(4):
+        put = jnp.where(lane == line + HEAD_DIM * h, 1.0, 0.0).astype(BF)
+        rel_ref[h] = nn(rel, put).astype(BF)
     source, valid = window_rows(t)
     valid_ref[...] = valid
     pick_rows = one_hot(source, 512)
@@ -432,7 +469,7 @@
 
     row_loop(norm_one)
     loads[1].wait()
-    down_q = HALF * nt(xn_s[...], a_q)
+    down_q = HALF * nt(xn_s[...], factor(0))
     dq_ext = jnp.where(lane_e == RANK, 1.0, down_q).astype(BF)
     d1_s[...] = dq_ext
     dqt_s[...] = down_q.T.astype(BF)
@@ -441,25 +478,31 @@
     def heads_forward(k, _):
         @pl.when(k == 1)
         def _():
-            wire.pack("c").wait_recv()
-            wire.have(1, range(3))
+            wire.pack("c", "wait")
+            wire.have(1, OF_Q)
+
+        ticks(wire, AT_SHARD, k)
+
+        @pl.when(k == 3)
+        def _():
+            wire.have(3, OF_Q)
+
+        x_q = nt(xn_s[...], wq[k])
 
         @pl.when(k == 2)
         def _():
-            for n in range(5):
-                wire.step(n)
+            wire.step("P0")
 
         @pl.when(k == 3)
         def _():
-            wire.pack("f").wait_recv()
-            wire.have(3, range(3))
-
-        qkv = nt(xn_s[...], wq[k]) + nn(d1_s[...], pack[k, :, 0 : 3 * LOC])
-        q_s[k, :, 0:LOC] = qkv[:, 0:LOC].astype(BF)
-        k_s[k, :, 0:LOC] = qkv[:, LOC : 2 * LOC].astype(BF)
-        v_s[k, :, 0:LOC] = qkv[:, 2 * LOC : 3 * LOC].astype(BF)
+            wire.pack("f", "wait")
+
+        for j, ref in enumerate((q_s, k_s, v_s)):
+            low_rank = nn(d1_s[...], pack_q[k, EXT * j : EXT * j + EXT, 0:LOC])
+            ref[k, :, 0:LOC] = (x_q[:, LOC * j : LOC * j + LOC] + low_rank).astype(BF)
 
         def window(w, _):
+            ticks(wire, AT_WINDOW, k * NW + w)
             rows = pl.ds(mult(w * PAD), PAD)
             shift = shift_ref[...]
             lane = lax.broadcasted_iota(jnp.int32, (PAD, 128), 1)
@@ -489,18 +532,18 @@
     lax.fori_loop(0, 4, heads_forward, 0)
 
     loads[3].wait()
-    wire.have(1, [3])
-    wire.step(5)
-    wire.have(3, [3])
+    wire.have(1, OF_P)
+    wire.have(3, OF_P)
+    loads[7].wait()
     down_p = jnp.zeros((R, RANK), F32)
     for k in range(4):
-        down_p += nt(att_s[k, :, 0:LOC], pack[k, 16:32, 2304 : 2304 + LOC])
+        down_p += nt(att_s[k, :, 0:LOC], pack_m[k, 16:32, HID : HID + LOC])
     down_p = HALF * down_p
     dp16 = down_p.astype(BF)
     dpt = down_p.T.astype(BF)
     for n in range(5):
         cols = slice(256 * n, 256 * n + 256)
-        total = nn(dp16, b_p[:RANK, cols]) + bias_p[:, cols]
+        total = nn(dp16, adp_ref[2, :, cols]) + bias_p[:, cols]
         for k in range(4):
             total += nn(att_s[k, :, 0:LOC], wp[k, :, cols])
         acc_a[:, cols] = total
@@ -512,7 +555,7 @@
         xn_s[rows, :] = (xhat * gain2 + shift2).astype(BF)
 
     row_loop(norm_two)
-    down_1 = HALF * nt(xn_s[...], a_1)
+    down_1 = HALF * nt(xn_s[...], factor(1))
     d1_s[...] = jnp.where(lane_e == RANK, 1.0, down_1).astype(BF)
     d1t_s[...] = down_1.T.astype(BF)
     loads[4].wait()
@@ -523,7 +566,7 @@
         g_s[:, cols] = nn(pick_rows, w2[0, 0:512, cols]).astype(BF)
     loads[6].start()
     valid = valid_ref[...]
-    up2 = HALF * valid * nt(g_s[...], b_2)
+    up2 = HALF * valid * nt(g_s[...], factor(3))
     up2_s[...] = up2.astype(BF)
     up2t_s[...] = up2.T.astype(BF)
     acc_a[...] = jnp.zeros((R, D), F32)
@@ -533,31 +576,15 @@
     loads[5].wait()
     loads[6].wait()
 
-    def hidden(i, _):
-        late = i - 10
-        k = jnp.where(i < 5, 0, jnp.where(i < 10, 1, 2 + lax.rem(late + 10, 2)))
-        c = jnp.where(i < 10, lax.rem(i, 5), (late + 10) // 2 - 5)
-
-        @pl.when(i == 5)
-        def _():
-            wire.have(1, range(4, NCH))
-
-        ticks(wire, {6: 2, 7: 6, 8: 9, 9: 10, 10: 10, 11: 12, 12: 14, 13: 16, 14: 18}, i)
-
-        @pl.when(i == 11)
-        def _():
-            wire.have(3, range(4, 8))
-
-        for j in range(5):
-
-            @pl.when(i == 11 + 2 * j)
-            def _():
-                wire.have(3, [8 + j])
-
+    def slice_of(i):
+        k = jnp.where(i < 5, 0, jnp.where(i < 10, 1, 2 + lax.rem(i, 2)))
+        c = jnp.where(i < 10, lax.rem(i, 5), i // 2 - 5)
         cols = pl.ds(mult(c * HC, HC), HC)
-        pcols = pl.ds(mult(1024 + c * HC, HC), HC)
-        acols = pl.ds(mult(2304 + c * HC, HC), HC)
-        pre = nn(xn_s[...], w1[k, :, cols]) + nn(d1_s[...], pack[k, :, pcols])
+        return k, cols, pack_m[k, :, pl.ds(mult(HID + c * HC, HC), HC)]
+
+    def hidden_values(i):
+        k, cols, a2 = slice_of(i)
+        pre = nn(xn_s[...], w1[k, :, cols]) + nn(d1_s[...], pack_m[k, :, cols])
         gauss = jnp.exp(-0.5 * pre * pre)
         t = 1.0 / (1.0 + (ERF_P * 0.5**0.5) * jnp.abs(pre))
         poly = ERF_A[4]
@@ -565,31 +592,58 @@
             poly = poly * t + a
         tail = (HALF * poly) * t * gauss
         phi = jnp.where(pre >= 0, 1.0 - tail, tail)
-        act = (pre * phi).astype(BF)
         slope = phi + pre * gauss * 0.3989422804014327
-        a2 = pack[k, :, acols]
+        dact = valid_ref[...] * nt(g_s[...], w2[k, cols, :]) + nn(up2_s[...], a2)
+        act_s[lax.rem(i, 2)] = (pre * phi).astype(BF)
+        dpre_s[lax.rem(i, 2)] = (dact * slope).astype(BF)
+
+    def hidden_sums(i):
+        k, cols, a2 = slice_of(i)
+        act, dpre = act_s[lax.rem(i, 2)], dpre_s[lax.rem(i, 2)]
         sum_1[k, RANK : 2 * RANK, cols] = nn(up2t_s[...], act)[:RANK].astype(BF)
+        sum_1[k, 0:RANK, cols] = nn(d1t_s[...], dpre)[:RANK].astype(BF)
         d2_s[...] += nt(act, a2)
-        dact = valid_ref[...] * nt(g_s[...], w2[k, cols, :]) + nn(up2_s[...], a2)
-        dpre = (dact * slope).astype(BF)
-        sum_1[k, 0:RANK, cols] = nn(d1t_s[...], dpre)[:RANK].astype(BF)
-        up1_s[...] += nt(dpre, pack[k, :, pcols])
+        up1_s[...] += nt(dpre, pack_m[k, :, cols])
         for n in range(5):
             out = slice(256 * n, 256 * n + 256)
             acc_a[:, out] += nn(act, w2[k, cols, out])
             acc_b[:, out] += nt(dpre, w1[k, out, cols])
+
+    def hidden(i, _):
+        @pl.when(i == 5)
+        def _():
+            wire.have(1, [*OF_1, *OF_2])
+
+        ticks(wire, AT_HIDDEN, i)
+
+        @pl.when(i == 11)
+        def _():
+            wire.have(3, OF_1)
+
+        for j in range(5):
+
+            @pl.when(i == 11 + 2 * j)
+            def _():
+                wire.have(3, [OF_2[j]])
+
+        hidden_sums(i - 1)
+        hidden_values(i)
         return 0
 
-    lax.fori_loop(0, 20, hidden, 0)
+    for what in AT_HIDDEN[0]:
+        wire.step(what)
+    hidden_values(0)
+    lax.fori_loop(1, 20, hidden, 0)
+    hidden_sums(19)
 
     wire.finish()
     wire.edge("ex", lambda n: x_hbm.at[0:n], lambda n: w1.at[0, ROWS : ROWS + n], False, "end")
     wire.edge("eg", lambda n: g_hbm.at[0:n], lambda n: w2.at[0, ROWS : ROWS + n], False, "end")
     wire.ready(done)
     d2 = HALF * d2_s[...]
-    d2b = d2.astype(BF)
+    d2b = d2[:, :RANK].astype(BF)
     up1 = HALF * up1_s[...]
-    up1b = up1.astype(BF)
+    up1b = up1[:, :RANK].astype(BF)
     rep_s[1] = nn((d2 * valid_ref[...]).T.astype(BF), g_s[...])[:RANK].astype(BF)
     rep_s[0] = nn(up1.T.astype(BF), xn_s[...])[:RANK].astype(BF)
     for k in range(4):
@@ -601,8 +655,8 @@
         total_1.first(k, all_1, "go")
     for n in range(5):
         cols = slice(256 * n, 256 * n + 256)
-        acc_a[:, cols] += nn(d2b, b_2[:, cols])
-        acc_b[:, cols] += nn(up1b, a_1[:, cols])
+        acc_a[:, cols] += nn(d2b, adp_ref[3, :, cols])
+        acc_b[:, cols] += nn(up1b, adp_ref[1, :, cols])
 
     def back_two(rows):
         mid = mid_s[rows, :]
@@ -621,16 +675,15 @@
         wire.edge(key, lambda n: src.at[R - n : R], to, True, do)
 
     swap_edge("eo", xn_s, w1, "go")
-    upp = HALF * nt(g_s[...], b_p)
+    upp = HALF * nt(g_s[...], factor(2))
     upp16 = upp[:, :RANK].astype(BF)
     uppt = upp.T.astype(BF)
     rep_s[1] = nn(dpt, g_s[...]).astype(BF)
-    acc_a[...] = jnp.zeros((R, D), F32)
-    upq_s[...] = jnp.zeros((R, EXT), F32)
+    d2_s[...] = jnp.zeros((R, EXT), F32)
     up2_s[:, 0:RANK] = upp16
     up2t_s[...] = uppt
 
-    put_out = pltpu.make_async_copy(w1.at[0, 0:ROWS], out_hbm, local.at[7])
+    put_out = pltpu.make_async_copy(w1.at[0, 0:ROWS], out_hbm, local.at[8])
 
     def heads_backward(step, _):
         k = lax.rem(step + 1, 4)
@@ -648,12 +701,15 @@
         @pl.when(step == 2)
         def _():
             total_1.add_second()
+            put_out.wait()
+            swap_edge("eo", xn_s, w1, "end")
+            row_loop(norm_one)
 
         @pl.when(step == 3)
         def _():
             total_1.add_third()
 
-        datt = nt(g_s[...], wp[k]) + nn(up2_s[:, 0:RANK], pack[k, 16:32, 2304 : 2304 + LOC])
+        datt = nt(g_s[...], wp[k]) + nn(up2_s[:, 0:RANK], pack_m[k, 16:32, HID : HID + LOC])
         datt_s[:, 0:LOC] = datt.astype(BF)
         sum_2[k, 0:RANK, 3 * LOC :] = nn(up2t_s[...], att_s[k, :, 0:LOC])[:RANK].astype(BF)
 
@@ -682,16 +738,9 @@
         lax.fori_loop(0, NW, window, 0)
         for j, ref in enumerate((q_s, k_s, v_s)):
             d = ref[k, :, 0:LOC]
-            b = pack[k, :, j * LOC : (j + 1) * LOC]
-            upq_s[...] += nt(d, b)
+            b = pack_q[k, EXT * j : EXT * j + EXT, 0:LOC]
+            d2_s[...] += nt(d, b)
             sum_2[k, 0:RANK, j * LOC : (j + 1) * LOC] = nn(dqt_s[...], d)[:RANK].astype(BF)
-        for n in range(5):
-            cols = slice(256 * n, 256 * n + 256)
-            total = acc_a[:, cols]
-            for j, ref in enumerate((q_s, k_s, v_s)):
-                total += nn(ref[k, :, 0:LOC], wq[k, j * LOC : (j + 1) * LOC, cols])
-            acc_a[:, cols] = total
-
         for kk in (1, 2, 3):
 
             @pl.when(k == kk)
@@ -701,44 +750,47 @@
         return 0
 
     lax.fori_loop(0, 4, heads_backward, 0)
-    puts = total_1.hand_out(split_1, whole_1, local.at[9:11])
-    put_out.wait()
-    swap_edge("eo", xn_s, w1, "end")
-
-    upq = HALF * upq_s[...]
-    upqb = upq.astype(BF)
-    upqt = upq.T.astype(BF)
-    for n in range(5):
-        cols = slice(256 * n, 256 * n + 256)
-        acc_a[:, cols] += nn(upqb, a_q[:, cols])
-
-    def back_one(rows):
-        ok = valid_ref[rows, :]
-        xhat, inv = stats(x_s[rows, :].astype(F32))
-        xn_s[rows, :] = (ok * (xhat * gain1 + shift1)).astype(BF)
-        back = norm_back(ok * acc_a[rows, :], xhat, inv, gain1)
-        g_s[rows, :] = (mid_s[rows, :] + back).astype(BF)
-
-    row_loop(back_one)
-    swap_edge("ef", g_s, w2, "go")
-    rep_s[0] = nn(upqt, xn_s[...])[:RANK].astype(BF)
+    puts = total_1.hand_out(split_1, whole_1, local.at[10:15])
+
+    upq = HALF * d2_s[...]
+    upqb = upq[:, :RANK].astype(BF)
+    rep_s[0] = nn(upq.T.astype(BF), xn_s[...])[:RANK].astype(BF)
     for k in range(4):
         sum_2[k, RANK:, 0 : D // 2] = half_of(rep_s, wire, k)
         sum_2[k, RANK:, D // 2 :] = jnp.zeros((RANK, D // 2), BF)
     low, high = pl.ds(0, RANK), pl.ds(RANK, RANK)
     for k in (1, 2, 3):
         total_2.first(k, high, "go")
-    total_2.add_first([low, high])
+
+    for n in range(5):
+        cols = slice(256 * n, 256 * n + 256)
+        total = nn(upqb, adp_ref[0, :, cols])
+        for k in range(4):
+            for j, ref in enumerate((q_s, k_s, v_s)):
+                total += nn(ref[k, :, 0:LOC], wq[k, j * LOC : (j + 1) * LOC, cols])
+        acc_a[:, cols] = total
+        if n == 1:
+            total_2.add_first([low, high])
+        if n == 3:
+            total_2.add_second()
+
+    def back_one(rows):
+        ok = valid_ref[rows, :]
+        xhat, inv = stats(x_s[rows, :].astype(F32))
+        back = norm_back(ok * acc_a[rows, :], xhat, inv, gain1)
+        g_s[rows, :] = (mid_s[rows, :] + back).astype(BF)
+
+    row_loop(back_one)
+    swap_edge("ef", g_s, w2, "go")
+    total_2.add_third()
     swap_edge("ef", g_s, w2, "wait")
     home = home_rows(t, g_s, w2.at[0, 512:672])
     for n in range(5):
         cols = slice(256 * n, 256 * n + 256)
         w2[0, 0:ROWS, cols] = home(cols)
-    put_grad = pltpu.make_async_copy(w2.at[0, 0:ROWS], grad_hbm, local.at[8])
+    put_grad = pltpu.make_async_copy(w2.at[0, 0:ROWS], grad_hbm, local.at[9])
     put_grad.start()
-    total_2.add_second()
-    total_2.add_third()
-    puts += total_2.hand_out(split_2, whole_2, local.at[11:13])
+    puts += total_2.hand_out(split_2, whole_2, local.at[15:20])
     for cp in puts:
         cp.wait()
     put_grad.wait()
@@ -747,19 +799,7 @@
     total_2.finish([low, high])
 
 
-def tables(rel_pos_h, rel_pos_w):
-    flip = np.zeros((2, 128, 2 * WIN - 1), np.float32)
-    for i in range(2 * WIN - 1):
-        flip[0, i, 2 * WIN - 2 - i] = 1
-        flip[1, 64 + i, 2 * WIN - 2 - i] = 1
-    rel = jnp.dot(flip[0].astype(BF), rel_pos_h) + jnp.dot(flip[1].astype(BF), rel_pos_w)
-    zero = lambda n: jnp.zeros((128, n), BF)
-    rel = jnp.stack(
-        [
-            jnp.concatenate([zero(80 * h), rel, zero(LP - 80 * h - 80)], axis=1)
-            for h in range(LOC // HEAD_DIM)
-        ]
-    )
+def tables():
     tok = np.arange(PAD)
     inside = tok < TOK
     row, col = tok // WIN, tok % WIN
@@ -772,7 +812,7 @@
     shift = np.where(np.arange(128)[None] < 64, 13 - row[:, None], 13 - col[:, None])
     shift = np.where(inside[:, None], shift, 0).astype(np.int32)
     key = np.where(inside, 0.0, -1e30).astype(np.float32)[None]
-    return rel, jnp.asarray(hot, BF), jnp.asarray(back.T, BF), jnp.asarray(shift), jnp.asarray(key)
+    return jnp.asarray(hot, BF), jnp.asarray(back.T, BF), jnp.asarray(shift), jnp.asarray(key)
 
 
 def call_kernel(images, args):
@@ -786,11 +826,11 @@
             sds((ROWS, D), BF),
             sds((ROWS, D), BF),
             sds((images * 3 * RANK, D), BF),
-            sds((4 * images * RANK, D // 2), BF),
+            sds((2 * images * RANK, D), BF),
             sds((images * 2 * RANK, D), BF),
-            sds((4 * images * RANK, D // 2), BF),
+            sds((2 * images * RANK, D), BF),
         ),
-        in_specs=[any_] * 7 + [vmem] * 7,
+        in_specs=[any_] * 8 + [vmem] * 8,
         out_specs=(any_,) * 6,
         scratch_shapes=[
             V((R, D), BF),
@@ -799,7 +839,9 @@
             V((4, LOC, D), BF),
             V((4, D, HID), BF),
             V((4, HID, D), BF),
-            V((4, EXT, PACK), BF),
+            V((4,) + PACK_Q, BF),
+            V((4,) + PACK_M, BF),
+            V((4, 128, LP), BF),
             V((R, D), BF),
             V((4, R, LP), BF),
             V((4, R, LP), BF),
@@ -810,11 +852,12 @@
             V((R, D), F32),
             V((R, D), F32),
             V((R, LP), BF),
+            V((2, R, HC), BF),
+            V((2, R, HC), BF),
             V((EXT, R), BF),
             V((EXT, R), BF),
             V((R, EXT), BF),
             V((R, EXT), BF),
-            V((R, EXT), F32),
             V((R, EXT), F32),
             V((R, EXT), F32),
             V((EXT, R), BF),
@@ -822,12 +865,12 @@
             V((4, 3 * RANK, D), BF),
             V((4, 2 * RANK, D), BF),
             V((2, RANK, D), BF),
-            pltpu.SemaphoreType.DMA((2, 12 * NCH + 60)),
-            pltpu.SemaphoreType.DMA((13,)),
+            pltpu.SemaphoreType.DMA((2, 8 * NCH + 63)),
+            pltpu.SemaphoreType.DMA((20,)),
             pltpu.SemaphoreType.REGULAR,
         ],
         compiler_params=pltpu.CompilerParams(
-            collective_id=0, has_side_effects=True, vmem_limit_bytes=66_500_000
+            collective_id=0, has_side_effects=True, vmem_limit_bytes=67_000_000
         ),
         name="block",
     )(*args)
@@ -871,32 +914,32 @@
 
     both = [jnp.pad(v, ((0, ROWS - v.shape[0]), (0, 0))) for v in (tokens, grad_out)]
     wq = jnp.transpose(qkv_weight, (1, 2, 0)).reshape(3 * LOC, D)
-    row = lambda v: v.reshape(1, -1)
-    bq = jnp.transpose(select(qkv_up), (0, 1, 2)).reshape(RANK, 3 * LOC)
-    pad_rows = lambda v, n: jnp.pad(v, ((0, n - v.shape[0]), (0, 0)))
-    bq = pad_rows(jnp.concatenate([bq, row(qkv_bias)]), EXT)
-    b1 = pad_rows(jnp.concatenate([select(lin1_up), row(lin1_bias)]), EXT)
-    low = jnp.concatenate(
-        [select(lin2_down).T, jnp.pad(select(proj_down).T, ((0, 0), (0, HID - LOC)))]
-    )
-    pack = jnp.concatenate([bq, jnp.zeros((EXT, 1024 - 3 * LOC), BF), b1, low], axis=1)
-    vecs = jnp.stack([norm1_gain, norm1_shift, norm2_gain, norm2_shift, proj_bias, lin2_bias])
-    vecs = jnp.pad(vecs.astype(F32), ((0, 2), (0, 0)))
+    rows = np.arange(EXT)[:, None]
+    pad_rows = lambda v: jnp.pad(v, ((0, EXT - RANK), (0, 0)))
+    up = select(jnp.transpose(qkv_up, (0, 2, 1, 3)))
+    up = jnp.pad(up, ((0, 0), (0, EXT - RANK), (0, 0)))
+    up = jnp.where(rows[None] == RANK, qkv_bias[:, None, :], up)
+    pack_q = up.reshape(PACK_Q)
+    b1 = jnp.where(rows == RANK, lin1_bias[None], pad_rows(select(lin1_up)))
+    low = jnp.pad(select(proj_down).T, ((RANK, 0), (0, HID - LOC)))
+    low = jnp.where(rows < RANK, pad_rows(select(lin2_down).T), low)
+    pack_m = jnp.concatenate([b1, low], axis=1)
+    vecs = jnp.zeros((8, D), BF)
+    for i, v in enumerate(
+        (norm1_gain, norm1_shift, norm2_gain, norm2_shift, proj_bias, lin2_bias)
+    ):
+        vecs = jnp.where(rows[:8] == i, v[None], vecs)
     adps = jnp.stack([select(qkv_down).T, select(lin1_down).T, select(proj_up), select(lin2_up)])
-    adps = jnp.pad(adps, ((0, 0), (0, EXT - RANK), (0, 0)))
-    rel, hot, back, shift, key = tables(rel_pos_h, rel_pos_w)
+    hot, back, shift, key = tables()
     out, grad, split_1, whole_1, split_2, whole_2 = call_kernel(
         images,
-        (*both, wq, proj_weight, lin1_weight, lin2_weight, pack,
-         vecs, adps, shift, rel, hot, back, key),
+        (*both, wq, proj_weight, lin1_weight, lin2_weight, pack_q, pack_m,
+         vecs, adps, shift, rel_pos_h, rel_pos_w, hot, back, key),
     )
 
     split_1 = split_1.reshape(images, 3 * RANK, D)
     split_2 = split_2.reshape(images, 2 * RANK, D)
-    whole_1, whole_2 = (
-        v.reshape(2, 2, images, RANK, D // 2).transpose(0, 2, 3, 1, 4).reshape(2, images, RANK, D)
-        for v in (whole_1, whole_2)
-    )
+    whole_1, whole_2 = (v.reshape(2, images, RANK, D) for v in (whole_1, whole_2))
 
     slots = jnp.arange(ADAPTERS)[:, None] == adapter_index[None]
 
@@ -909,12 +952,13 @@
         return total
 
     swap = lambda v: jnp.swapaxes(v, 1, 2)
-    up_q = split_2[:, :RANK, : 3 * LOC].reshape(images, RANK, 3, LOC)
+    up_q = [split_2[:, :RANK, LOC * j : LOC * j + LOC] for j in range(3)]
+    up_q = jnp.stack(up_q, axis=1)
     return (
         out[:row_count],
         grad[:row_count],
         swap(to_slots(whole_2[0])),
-        to_slots(up_q),
+        swap(to_slots(up_q)),
         swap(to_slots(split_2[:, :RANK, 3 * LOC :])),
         to_slots(whole_2[1]),
         swap(to_slots(whole_1[0])),

time: 264 us -> 222 us (0.84)
  Pallas kernels: 230 us -> 193 us
  local copies, waits for them, and re-layouts: 16.6 us -> 11.2 us
    pallas_call x1, Pallas kernels: 230 us -> 193 us  [call_kernel(): pl.pallas_call(functools.partial(kernel, images), out_shape=(sds((ROWS, D...]
    another operation x7 -> x0, local copies, waits for them, and re-layouts: 4.2 us -> none  [on_device(): jnp.stack([norm1_gain, norm1_shift, norm2_gain, norm2_shift, proj_bias, l...]
    select_n x0 -> x3, other arithmetic: none -> 3.7 us  [the longest x1 1.52 us: on_device(): vecs = jnp.where(rows[:8] == i, v[None], vecs)]
where the time goes in v3:
time: 222 us; the launch traced here: 221 us
  Pallas kernels  193 us (87%)
  other arithmetic  13.6 us (6%)
  local copies, waits for them, and re-layouts  11.2 us (5%)
  between operations  2.76 us (1%)
    pallas_call x1, Pallas kernels, call_kernel(): pl.pallas_call(functools.partial(kernel, images), out_shape=(sds((ROWS, D...  193 us
    add x4, other arithmetic, to_slots(): total = total + jnp.where(hit, v[i][None], 0.0)  4.53 us

profile of v3, /device:TPU:0, one launch (start us, length us, event | category | flops | bytes accessed | tf_op | source)
XLA Modules:
  0.0 220.8 jit_solution(7731076659016925700)
XLA Ops:
  0.6 0.0 copy-start
  0.7 1.4 fusion
  4.0 0.7 iota_compare_fusion
  4.7 0.7 dynamic-slice_bitcast_fusion.5
  5.4 1.5 select_select_fusion.vec_ref
  7.0 0.8 dynamic-slice_bitcast_fusion.4
  7.7 1.4 pad_select_fusion.2
  9.1 0.8 dynamic-slice_bitcast_fusion.3
  9.9 0.8 dynamic-slice_bitcast_fusion.2
  10.7 0.8 pad_select_fusion
  11.5 0.7 pad_maximum_fusion.pm_hbm
  12.2 0.8 dynamic-slice_bitcast_fusion
  13.0 0.8 constant_dynamic-slice_fusion
  13.8 0.7 pad_maximum_fusion.1.adp_ref
  14.5 2.1 pad.22.x_hbm
  16.6 0.0 copy-done
  16.6 1.0 pad.23.g_hbm
  17.6 193.2 %block.1 = (bf16[352,1280]{1,0:T(8,128)(2,1)}, bf16[352,1280]{1,0:T(8,128)(2,1)}, bf16[96,1280]{1,0:T(8,128)(2,1)}, bf16[64,1280]{1,0:T(8,128)(2,1)}, bf16[64,12...) custom-call(bf16[352,1280]{1,0:T(8,128)(2,1)} %pad.22.x_hbm, bf16[352,1280]{1,0:T(8,128)(2,1)} %pad.23.g_hbm, ...), custom_call_target="tpu_custom_call" | custom-call | tf_op jit(solution)/shard_map/block/pallas_call | solution.py:823
  210.9 0.0 copy-start.2
  210.9 0.0 copy-start.3
  210.9 0.0 copy-start.1
  210.9 2.2 %slice.116 = bf16[343,1280]{1,0:T(8,128)(2,1)} slice(bf16[352,1280]{1,0:T(8,128)(2,1)} %get-tuple-element.16), slice={[0:343], [0:1280]} | slice | bytes 1756160 | tf_op jit(solution)/shard_map/slice | solution.py:958
  213.1 0.9 slice_convert_fusion.6
  214.1 0.8 select_add_fusion.7
  214.9 1.0 slice_convert_fusion.4
  215.9 0.0 copy-done.2
  216.0 0.0 copy-done.3
  216.1 0.9 select_add_fusion.6
  217.0 0.0 copy-done.1
  217.0 1.0 slice.117
  218.0 1.4 select_add_fusion
  219.4 1.4 select_add_fusion.1
  (12 shorter events, 0.2 us)
Async XLA Ops:
  0.6 16.0 %copy-start = (bf16[343,1280]{1,0:T(8,128)(2,1)S(1)}, bf16[343,1280]{1,0:T(8,128)(2,1)}, u32[]{:S(2)}) copy-start(bf16[343,1280]{1,0:T(8,128)(2,1)} %param.39) | copy-start | bytes 2634244
  210.9 5.0 %copy-start.2 = (bf16[64,1280]{1,0:T(8,128)(2,1)S(1)}, bf16[64,1280]{1,0:T(8,128)(2,1)}, u32[]{:S(2)}) copy-start(bf16[64,1280]{1,0:T(8,128)(2,1)} %get-tuple-element.20) | copy-start | bytes 491524
  210.9 5.1 %copy-start.3 = (bf16[96,1280]{1,0:T(8,128)(2,1)S(1)}, bf16[96,1280]{1,0:T(8,128)(2,1)}, u32[]{:S(2)}) copy-start(bf16[96,1280]{1,0:T(8,128)(2,1)} %get-tuple-element.21) | copy-start | bytes 737284
  210.9 6.1 %copy-start.1 = (bf16[352,1280]{1,0:T(8,128)(2,1)S(1)}, bf16[352,1280]{1,0:T(8,128)(2,1)}, u32[]{:S(2)}) copy-start(bf16[352,1280]{1,0:T(8,128)(2,1)} %get-tuple-element.17) | copy-start | bytes 2703364

commit v4 on v3

--- a/solution.py
+++ b/solution.py
@@ -385,15 +385,9 @@
                 wire.step(what)
 
 
-AT_WINDOW = {
-    1: ("A0",), 2: ("A1", "B0"), 3: ("A2", "B1", "C0"), 5: ("A5",), 6: ("B5", "A6"), 7: ("C5",),
-}
-AT_SHARD = {2: ("A3", "B2", "C1", "A4", "B3", "C2", "B4", "C3", "C4")}
-AT_HIDDEN = {
-    0: ("A7", "B6", "A8"), 1: ("C6", "B7"), 3: ("A9", "B8", "C7"), 5: ("A10", "B9", "C8"),
-    7: ("A11", "B10", "C9"), 10: ("A12", "B11", "C10"), 12: ("A13", "B12", "C11"),
-    14: ("B13", "C12", "A14"), 16: ("B14", "C13"), 17: ("C14",),
-}
+AT_WINDOW = {1: ('A0',), 2: ('A1', 'B0'), 3: ('A2', 'B1', 'C0'), 5: ('A5',), 6: ('B5', 'A6'), 7: ('C5',)}
+AT_SHARD = {2: ('A3', 'B2', 'C1', 'A4', 'B3', 'C2', 'B4', 'C3', 'C4')}
+AT_HIDDEN = {0: ('C6', 'B7', 'A8'), 2: ('A9', 'B8', 'C7'), 4: ('A10', 'B9', 'C8'), 6: ('A11', 'B10', 'C9'), 8: ('A12', 'B11', 'C10'), 10: ('A13', 'B12', 'C11'), 12: ('A14', 'B13', 'C12'), 14: ('B14', 'C13'), 16: ('C14',)}
 
 
 def kernel(
@@ -534,6 +528,8 @@
     loads[3].wait()
     wire.have(1, OF_P)
     wire.have(3, OF_P)
+    wire.step("A7")
+    wire.step("B6")
     loads[7].wait()
     down_p = jnp.zeros((R, RANK), F32)
     for k in range(4):
@@ -547,6 +543,7 @@
         for k in range(4):
             total += nn(att_s[k, :, 0:LOC], wp[k, :, cols])
         acc_a[:, cols] = total
+
 
     def norm_two(rows):
         mid = x_s[rows, :].astype(F32) + valid_ref[rows, :] * acc_a[rows, :]
@@ -876,6 +873,111 @@
     )(*args)
 
 
+def before_kernel(
+    pick, x_ref, g_ref, q_down, q_up, p_down, p_up, down_1, up_1, down_2, up_2, q_bias, vec_ref,
+    x_out, g_out, pack_q, pack_m, adp_ref,
+):
+    rows = x_ref.shape[0]
+    for src, dst in ((x_ref, x_out), (g_ref, g_out)):
+        dst[0:rows, :] = src[...]
+        dst[rows:, :] = jnp.zeros((ROWS - rows, D), BF)
+    for i, ref in enumerate((q_down, down_1, p_up, up_2)):
+        adp_ref[i] = ref[0]
+    line = lax.broadcasted_iota(jnp.int32, (RANK, 1), 0)
+
+    def bias_rows(bias):
+        return jnp.where(line == 0, bias, 0.0).astype(BF)
+
+    biases, vecs = q_bias[...].astype(F32), vec_ref[...].astype(F32)
+    for j in range(3):
+        pack_q[EXT * j : EXT * j + RANK, :] = q_up[0, j]
+        pack_q[EXT * j + RANK : EXT * j + EXT, :] = bias_rows(biases[j : j + 1, :])
+    pack_m[0:RANK, 0:HID] = up_1[0]
+    pack_m[RANK:EXT, 0:HID] = bias_rows(vecs[6:7, :])
+    pack_m[0:RANK, HID:] = down_2[0]
+    pack_m[RANK:EXT, HID : HID + LOC] = p_down[0]
+    pack_m[RANK:EXT, HID + LOC :] = jnp.zeros((RANK, HID - LOC), BF)
+
+
+def call_before(pick, args):
+    sds = jax.ShapeDtypeStruct
+
+    def spec(v):
+        if v.ndim > 2:
+            return pl.BlockSpec(
+                (1,) + v.shape[1:], lambda i, p: (p[0],) + (0,) * (v.ndim - 1)
+            )
+        return pl.BlockSpec(v.shape, lambda i, p: (0, 0))
+
+    outs = (
+        sds((ROWS, D), BF), sds((ROWS, D), BF), sds(PACK_Q, BF), sds(PACK_M, BF),
+        sds((4, RANK, D), BF),
+    )
+    return pl.pallas_call(
+        before_kernel,
+        out_shape=outs,
+        grid_spec=pltpu.PrefetchScalarGridSpec(
+            num_scalar_prefetch=1,
+            grid=(1,),
+            in_specs=[spec(v) for v in args],
+            out_specs=tuple(
+                pl.BlockSpec(v.shape, lambda i, p, n=len(v.shape): (0,) * n) for v in outs
+            ),
+        ),
+        compiler_params=pltpu.CompilerParams(vmem_limit_bytes=66_500_000),
+        name="before",
+    )(pick, *args)
+
+
+def after_kernel(
+    images, pick, out_ref, grad_ref, split_1, whole_1, split_2, whole_2,
+    out, grad, q_down, q_up, p_down, p_up, down_1, up_1, down_2, up_2,
+):
+    out[...] = out_ref[0 : out.shape[0], :]
+    grad[...] = grad_ref[0 : out.shape[0], :]
+
+    def slot(a, _):
+        hits = [jnp.where(pick[i] == a, 1.0, 0.0) for i in range(images)]
+
+        def total(ref, first, step, cols=slice(None)):
+            v = 0.0
+            for i in range(images):
+                at = first + i * step
+                v = v + hits[i] * ref[at : at + RANK, cols].astype(F32)
+            return v
+
+        up_1[a] = total(split_1, 0, 3 * RANK)
+        down_2[a] = total(split_1, RANK, 3 * RANK)
+        down_1[a] = total(whole_1, 0, RANK)
+        up_2[a] = total(whole_1, images * RANK, RANK)
+        q_down[a] = total(whole_2, 0, RANK)
+        p_up[a] = total(whole_2, images * RANK, RANK)
+        for j in range(3):
+            q_up[a, j] = total(split_2, 0, 2 * RANK, slice(LOC * j, LOC * j + LOC))
+        p_down[a] = total(split_2, 0, 2 * RANK, slice(3 * LOC, 4 * LOC))
+        return 0
+
+    lax.fori_loop(0, ADAPTERS, slot, 0)
+
+
+def call_after(images, row_count, pick, args):
+    sds = jax.ShapeDtypeStruct
+    full = sds((ADAPTERS, RANK, D), F32)
+    vmem = pl.BlockSpec(memory_space=pltpu.VMEM)
+    return pl.pallas_call(
+        functools.partial(after_kernel, images),
+        out_shape=(
+            sds((row_count, D), BF), sds((row_count, D), BF),
+            full, sds((ADAPTERS, 3, RANK, LOC), F32), sds((ADAPTERS, RANK, LOC), F32), full,
+            full, full, full, full,
+        ),
+        in_specs=[pl.BlockSpec(memory_space=pltpu.SMEM)] + [vmem] * 6,
+        out_specs=(vmem,) * 10,
+        compiler_params=pltpu.CompilerParams(vmem_limit_bytes=66_500_000),
+        name="after",
+    )(pick, *args)
+
+
 def on_device(
     tokens,
     grad_out,
@@ -907,64 +1009,41 @@
     row_count = tokens.shape[0]
     dp_place = lax.axis_index("dp")
     image = dp_place // GROUP
-    pick = jnp.sum(jnp.where(jnp.arange(images) == image, adapter_index, 0))
-
-    def select(table_all):
-        return lax.dynamic_index_in_dim(table_all, pick, 0, keepdims=False)
-
-    both = [jnp.pad(v, ((0, ROWS - v.shape[0]), (0, 0))) for v in (tokens, grad_out)]
+    pick = lax.dynamic_slice_in_dim(adapter_index, image, 1)
+
     wq = jnp.transpose(qkv_weight, (1, 2, 0)).reshape(3 * LOC, D)
-    rows = np.arange(EXT)[:, None]
-    pad_rows = lambda v: jnp.pad(v, ((0, EXT - RANK), (0, 0)))
-    up = select(jnp.transpose(qkv_up, (0, 2, 1, 3)))
-    up = jnp.pad(up, ((0, 0), (0, EXT - RANK), (0, 0)))
-    up = jnp.where(rows[None] == RANK, qkv_bias[:, None, :], up)
-    pack_q = up.reshape(PACK_Q)
-    b1 = jnp.where(rows == RANK, lin1_bias[None], pad_rows(select(lin1_up)))
-    low = jnp.pad(select(proj_down).T, ((RANK, 0), (0, HID - LOC)))
-    low = jnp.where(rows < RANK, pad_rows(select(lin2_down).T), low)
-    pack_m = jnp.concatenate([b1, low], axis=1)
     vecs = jnp.zeros((8, D), BF)
     for i, v in enumerate(
-        (norm1_gain, norm1_shift, norm2_gain, norm2_shift, proj_bias, lin2_bias)
+        (norm1_gain, norm1_shift, norm2_gain, norm2_shift, proj_bias, lin2_bias, lin1_bias)
     ):
-        vecs = jnp.where(rows[:8] == i, v[None], vecs)
-    adps = jnp.stack([select(qkv_down).T, select(lin1_down).T, select(proj_up), select(lin2_up)])
+        vecs = jnp.where(np.arange(8)[:, None] == i, v[None], vecs)
+    swap = lambda v: jnp.swapaxes(v, 1, 2)
+    x, g, pack_q, pack_m, adps = call_before(
+        pick,
+        (tokens, grad_out, swap(qkv_down), swap(qkv_up), swap(proj_down), proj_up,
+         swap(lin1_down), lin1_up, swap(lin2_down), lin2_up, qkv_bias, vecs),
+    )
     hot, back, shift, key = tables()
     out, grad, split_1, whole_1, split_2, whole_2 = call_kernel(
         images,
-        (*both, wq, proj_weight, lin1_weight, lin2_weight, pack_q, pack_m,
+        (x, g, wq, proj_weight, lin1_weight, lin2_weight, pack_q, pack_m,
          vecs, adps, shift, rel_pos_h, rel_pos_w, hot, back, key),
     )
 
-    split_1 = split_1.reshape(images, 3 * RANK, D)
-    split_2 = split_2.reshape(images, 2 * RANK, D)
-    whole_1, whole_2 = (v.reshape(2, images, RANK, D) for v in (whole_1, whole_2))
-
-    slots = jnp.arange(ADAPTERS)[:, None] == adapter_index[None]
-
-    def to_slots(v):
-        v = v.astype(F32)
-        total = 0.0
-        for i in range(images):
-            hit = slots[:, i].reshape((-1,) + (1,) * (v.ndim - 1))
-            total = total + jnp.where(hit, v[i][None], 0.0)
-        return total
-
-    swap = lambda v: jnp.swapaxes(v, 1, 2)
-    up_q = [split_2[:, :RANK, LOC * j : LOC * j + LOC] for j in range(3)]
-    up_q = jnp.stack(up_q, axis=1)
+    (out, grad, q_down, q_up, p_down, p_up, down_1, up_1, down_2, up_2) = call_after(
+        images, row_count, adapter_index, (out, grad, split_1, whole_1, split_2, whole_2)
+    )
     return (
-        out[:row_count],
-        grad[:row_count],
-        swap(to_slots(whole_2[0])),
-        swap(to_slots(up_q)),
-        swap(to_slots(split_2[:, :RANK, 3 * LOC :])),
-        to_slots(whole_2[1]),
-        swap(to_slots(whole_1[0])),
-        to_slots(split_1[:, :RANK]),
-        swap(to_slots(split_1[:, RANK : 2 * RANK])),
-        to_slots(whole_1[1]),
+        out,
+        grad,
+        swap(q_down),
+        swap(q_up),
+        swap(p_down),
+        p_up,
+        swap(down_1),
+        up_1,
+        swap(down_2),
+        up_2,
     )
 
 

time: 222 us -> 201 us (0.905)
  other arithmetic: 13.6 us -> 1.53 us
  local copies, waits for them, and re-layouts: 11.2 us -> 1.24 us
  Pallas kernels: 193 us -> 197 us
    pallas_call x0 -> x2, Pallas kernels: none -> 9.31 us  [the longest x1 5.73 us: call_after(): pl.pallas_call(functools.partial(after_kernel, images), out_shape=(sds((r...]
    pallas_call x1, Pallas kernels: 193 us -> 188 us  [call_kernel(): pl.pallas_call(functools.partial(kernel, images), out_shape=(sds((ROWS, D...]
    add x4 -> x0, other arithmetic: 4.53 us -> none  [to_slots(): total = total + jnp.where(hit, v[i][None], 0.0)]
    slice x4 -> x0, local copies, waits for them, and re-layouts: 3.23 us -> none  [the longest x1 2.23 us: on_device(): out[:row_count]]
    pad x2 -> x0, local copies, waits for them, and re-layouts: 3.17 us -> none  [on_device(): jnp.pad(v, ((0, ROWS - v.shape[0]), (0, 0)))]
where the time goes in v4:
time: 201 us
  Pallas kernels  197 us (98%)
    pallas_call x1, Pallas kernels, call_kernel(): pl.pallas_call(functools.partial(kernel, images), out_shape=(sds((ROWS, D...  188 us
    pallas_call x1, Pallas kernels, call_after(): pl.pallas_call(functools.partial(after_kernel, images), out_shape=(sds((r...  5.73 us

profile of v4, /device:TPU:0, one launch (start us, length us, event | category | flops | bytes accessed | tf_op | source)
XLA Modules:
  0.0 200.5 jit_solution(17810373434509924195)
XLA Ops:
  0.7 1.2 dynamic_slice.3.pick
  1.9 1.5 select_select_fusion.vec_ref
  3.4 3.6 %before.1 = (bf16[352,1280]{1,0:T(8,128)(2,1)}, bf16[352,1280]{1,0:T(8,128)(2,1)}, bf16[96,320]{1,0:T(8,128)(2,1)}, bf16[32,2560]{1,0:T(8,128)(2,1)}, bf16[4,16,1280]{2,1,0:T(8,128)(2,1)}) custom-call(s32[1]{0:T(128)} %dynamic_slice.3.pick, bf16[343,1280]{1,0:T(8,128)(2,1)} %x_ref.1, bf16[343,1280]{1,0:T(8,128)(2,1)} %g_ref.1, ...), custom_call_target="tpu_custom_call" | custom-call | tf_op jit(solution)/shard_map/before/pallas_call | solution.py:916
  7.0 187.8 %block.1 = (bf16[352,1280]{1,0:T(8,128)(2,1)}, bf16[352,1280]{1,0:T(8,128)(2,1)}, bf16[96,1280]{1,0:T(8,128)(2,1)}, bf16[64,1280]{1,0:T(8,128)(2,1)}, bf16[64,12...) custom-call(bf16[352,1280]{1,0:T(8,128)(2,1)} %get-tuple-element.31.x_hbm, bf16[352,1280]{1,0:T(8,128)(2,1)} %get-tuple-element.32.g_hbm, ...), custom_call_target="tpu_custom_call" | custom-call | tf_op jit(solution)/shard_map/block/pallas_call | solution.py:820
  194.8 5.7 %after.1 = (bf16[343,1280]{1,0:T(8,128)(2,1)}, bf16[343,1280]{1,0:T(8,128)(2,1)}, f32[8,16,1280]{2,1,0:T(8,128)}, f32[8,3,16,320]{3,2,1,0:T(8,128)}, f32[8,16,32...) custom-call(s32[2]{0:T(128)} %pick.1, ...), custom_call_target="tpu_custom_call" | custom-call | tf_op jit(solution)/shard_map/after/pallas_call | solution.py:967

commit v5 on v4

--- a/solution.py
+++ b/solution.py
@@ -168,8 +168,8 @@
         self.pack("c", "go")
         for c in range(NCH):
             if c == OF_P[0]:
+                after_heads()
                 self.pack("y", "go")
-                after_heads()
             self.piece(c, "y1").start()
             self.piece(c, "y2").start()
             self.piece(c, "s").start()
@@ -386,7 +386,8 @@
 
 
 AT_WINDOW = {1: ('A0',), 2: ('A1', 'B0'), 3: ('A2', 'B1', 'C0'), 5: ('A5',), 6: ('B5', 'A6'), 7: ('C5',)}
-AT_SHARD = {2: ('A3', 'B2', 'C1', 'A4', 'B3', 'C2', 'B4', 'C3', 'C4')}
+AT_SHARD = {2: ("A3", "B2", "C1", "A4", "B3", "C2")}
+AFTER_GRADIENT = ("B4", "C3", "C4")
 AT_HIDDEN = {0: ('C6', 'B7', 'A8'), 2: ('A9', 'B8', 'C7'), 4: ('A10', 'B9', 'C8'), 6: ('A11', 'B10', 'C9'), 8: ('A12', 'B11', 'C10'), 10: ('A13', 'B12', 'C11'), 12: ('A14', 'B13', 'C12'), 14: ('B14', 'C13'), 16: ('C14',)}
 
 
@@ -469,6 +470,22 @@
     dqt_s[...] = down_q.T.astype(BF)
     loads[2].wait()
 
+    def output_gradient():
+        loads[4].wait()
+        wire.edge("eg", lambda n: g_hbm.at[0:n], lambda n: w2.at[0, ROWS : ROWS + n], False, "wait")
+        picks = one_hot(window_rows(t)[0], 512)
+        for n in range(5):
+            cols = slice(256 * n, 256 * n + 256)
+            g_s[:, cols] = nn(picks, w2[0, 0:512, cols]).astype(BF)
+        loads[6].start()
+        ok = valid_ref[...]
+        up2 = HALF * ok * nt(g_s[...], factor(3))
+        up2_s[...] = up2.astype(BF)
+        up2t_s[...] = up2.T.astype(BF)
+        acc_b[...] = jnp.zeros((R, D), F32)
+        d2_s[...] = jnp.zeros((R, EXT), F32)
+        up1_s[...] = jnp.zeros((R, EXT), F32)
+
     def heads_forward(k, _):
         @pl.when(k == 1)
         def _():
@@ -476,6 +493,12 @@
             wire.have(1, OF_Q)
 
         ticks(wire, AT_SHARD, k)
+
+        @pl.when(k == 2)
+        def _():
+            output_gradient()
+            for what in AFTER_GRADIENT:
+                wire.step(what)
 
         @pl.when(k == 3)
         def _():
@@ -555,21 +578,7 @@
     down_1 = HALF * nt(xn_s[...], factor(1))
     d1_s[...] = jnp.where(lane_e == RANK, 1.0, down_1).astype(BF)
     d1t_s[...] = down_1.T.astype(BF)
-    loads[4].wait()
-    wire.edge("eg", lambda n: g_hbm.at[0:n], lambda n: w2.at[0, ROWS : ROWS + n], False, "wait")
-    pick_rows = one_hot(window_rows(t)[0], 512)
-    for n in range(5):
-        cols = slice(256 * n, 256 * n + 256)
-        g_s[:, cols] = nn(pick_rows, w2[0, 0:512, cols]).astype(BF)
-    loads[6].start()
-    valid = valid_ref[...]
-    up2 = HALF * valid * nt(g_s[...], factor(3))
-    up2_s[...] = up2.astype(BF)
-    up2t_s[...] = up2.T.astype(BF)
     acc_a[...] = jnp.zeros((R, D), F32)
-    acc_b[...] = jnp.zeros((R, D), F32)
-    d2_s[...] = jnp.zeros((R, EXT), F32)
-    up1_s[...] = jnp.zeros((R, EXT), F32)
     loads[5].wait()
     loads[6].wait()
 

time: 201 us -> 200 us (level)
  no operation moved by 1% of the time
where the time goes in v5:
time: 200 us
  Pallas kernels  196 us (98%)
    pallas_call x1, Pallas kernels, call_kernel(): pl.pallas_call(functools.partial(kernel, images), out_shape=(sds((ROWS, D...  187 us
    pallas_call x1, Pallas kernels, call_after(): pl.pallas_call(functools.partial(after_kernel, images), out_shape=(sds((r...  5.73 us

profile of v5, /device:TPU:0, one launch (start us, length us, event | category | flops | bytes accessed | tf_op | source)
XLA Modules:
  0.0 199.7 jit_solution(16577810725996843813)
XLA Ops:
  0.7 1.2 dynamic_slice.3.pick
  1.9 1.5 select_select_fusion.vec_ref
  3.4 3.6 %before.1 = (bf16[352,1280]{1,0:T(8,128)(2,1)}, bf16[352,1280]{1,0:T(8,128)(2,1)}, bf16[96,320]{1,0:T(8,128)(2,1)}, bf16[32,2560]{1,0:T(8,128)(2,1)}, bf16[4,16,1280]{2,1,0:T(8,128)(2,1)}) custom-call(s32[1]{0:T(128)} %dynamic_slice.3.pick, bf16[343,1280]{1,0:T(8,128)(2,1)} %x_ref.1, bf16[343,1280]{1,0:T(8,128)(2,1)} %g_ref.1, ...), custom_call_target="tpu_custom_call" | custom-call | tf_op jit(solution)/shard_map/before/pallas_call | solution.py:925
  7.0 187.0 %block.1 = (bf16[352,1280]{1,0:T(8,128)(2,1)}, bf16[352,1280]{1,0:T(8,128)(2,1)}, bf16[96,1280]{1,0:T(8,128)(2,1)}, bf16[64,1280]{1,0:T(8,128)(2,1)}, bf16[64,12...) custom-call(bf16[352,1280]{1,0:T(8,128)(2,1)} %get-tuple-element.31.x_hbm, bf16[352,1280]{1,0:T(8,128)(2,1)} %get-tuple-element.32.g_hbm, ...), custom_call_target="tpu_custom_call" | custom-call | tf_op jit(solution)/shard_map/block/pallas_call | solution.py:829
  194.0 5.7 %after.1 = (bf16[343,1280]{1,0:T(8,128)(2,1)}, bf16[343,1280]{1,0:T(8,128)(2,1)}, f32[8,16,1280]{2,1,0:T(8,128)}, f32[8,3,16,320]{3,2,1,0:T(8,128)}, f32[8,16,32...) custom-call(s32[2]{0:T(128)} %pick.1, ...), custom_call_target="tpu_custom_call" | custom-call | tf_op jit(solution)/shard_map/after/pallas_call | solution.py:976
